TPU v7x, 256 devices: a whole 4x4x8 slice. The times are simulated.
256 devices in a mesh: wide: 64 (over z, x, core), narrow: 4 (over y).
Axes of the slice: x: 4, y: 4, z: 8, core: 2. Of those that a mesh axis runs over, the one named last changes fastest.
Arguments:
- embeddings: bfloat16 [524288, 1536], P(('wide', 'narrow')), may hold values from -400 to 400
- test_matrix: bfloat16 [1536, 256], replicated, may hold values from -0.15625 to 0.15625
Outputs:
- basis: float32 [524288, 256], P(('wide', 'narrow'))
- loadings: float32 [1536, 256], P('wide')
All inputs are finite; a program needn't handle non-finite values.
Results may differ from a plain program's by a relative error of at most 0.0043.
Values sent between devices are 32-bit elements; how exact they have to be, the bound alone decides.
No kernel may reach another device: no remote copies, remote signals or barrier semaphores. Data moves between devices by JAX's collectives and lax.ppermute only.
A program may use at most 64 MiB of HBM per device.

v0:
```python
import jax
import jax.numpy as jnp
from jax import lax
from jax.sharding import PartitionSpec as P


def from_partner(x, axis, bit):
    return lax.ppermute(x, axis, [(i, i ^ 1 << bit) for i in range(lax.axis_size(axis))])


def factor_inverse(gram):
    order = gram.shape[0]
    lower = jnp.linalg.cholesky(gram)
    identity = jnp.eye(order, dtype=gram.dtype)
    return jax.scipy.linalg.solve_triangular(lower, identity, trans="T", lower=True)


def body(embeddings, test_matrix):
    n_wide = lax.axis_size("wide")
    n_narrow = lax.axis_size("narrow")
    rows_total = embeddings.shape[0] * n_wide * n_narrow
    rank_cols = test_matrix.shape[1]
    sketch = jnp.dot(embeddings, test_matrix, preferred_element_type=jnp.float32).astype(
        jnp.bfloat16
    )
    local_gram = (
        lax.dot_general(
            sketch, sketch, (((0,), (0,)), ((), ())), preferred_element_type=jnp.float32
        )
        / rows_total
    )
    gram_sum = local_gram
    for level_bit in range(n_wide.bit_length() - 1):
        gram_sum = gram_sum + from_partner(gram_sum, "wide", level_bit)
    for level_bit in range(n_narrow.bit_length() - 1):
        gram_sum = gram_sum + from_partner(gram_sum, "narrow", level_bit)
    inverse = factor_inverse(gram_sum)
    basis_rows = jnp.dot(sketch.astype(jnp.float32), inverse, precision=lax.Precision.HIGHEST)
    cross_terms = lax.dot_general(
        embeddings, sketch, (((0,), (0,)), ((), ())), preferred_element_type=jnp.float32
    )
    cross_terms = jnp.dot(cross_terms, inverse, precision=lax.Precision.HIGHEST) / rows_total
    feature_count = cross_terms.shape[0]
    owned_cols = feature_count // n_wide
    pieces = lax.all_to_all(
        cross_terms.reshape(n_wide, owned_cols, rank_cols),
        "wide",
        split_axis=0,
        concat_axis=0,
        tiled=True,
    )
    owned_rows = lax.psum(jnp.sum(pieces, axis=0), "narrow")
    return (basis_rows, owned_rows)


def solution(mesh):
    in_specs = (P(("wide", "narrow"), None), P())
    out_specs = (P(("wide", "narrow"), None), P("wide", None))
    return jax.shard_map(body, mesh=mesh, in_specs=in_specs, out_specs=out_specs, check_vma=False)
```

profile of v0, /device:TPU:4, one launch (start us, length us, event | category | flops | bytes accessed | tf_op | source)
XLA Modules:
  0.0 228.5 jit_solution(2681915546240139798)
XLA Ops:
  1.8 4.6 %convolution_convert_fusion = bf16[2048,256]{1,0:T(8,128)(2,1)S(1)} fusion(bf16[2048,1536]{1,0:T(8,128)(2,1)} %param.2, bf16[1536,256]{1,0:T(8,128)(2,1)S(1)} %copy-done), kind=kOutput, calls=%fused_computation.3 | convolution fusion | flops 1611137024 | bytes 8126464 | tf_op jit(solution)/shard_map/dot_general | solution.py:23
  9.8 7.1 %collective-permute-done.1 = f32[256,256]{0,1:T(8,128)S(1)} collective-permute-done((f32[256,256]{0,1:T(8,128)S(1)}, f32[256,256]{0,1:T(8,128)S(1)}, u32[]{:S(2)}, u32[]{:S(2)}) %collective-permute-start.1) | collective-permute-done | bytes 262176 | tf_op jit(solution)/shard_map/ppermute | solution.py:8
  17.0 2.3 %collective-permute-start.2 = (f32[256,256]{0,1:T(8,128)S(1)}, f32[256,256]{0,1:T(8,128)S(1)}, u32[]{:S(2)}, u32[]{:S(2)}) collective-permute-start(f32[256,256]{0,1:T(8,128)S(1)} %add.50), channel_id=1, source_target_pairs={{0,16},{4,20},{8,24},{12,28},{16,0},{20,4},{24,8},{28,12},{32,48},... | collective-permute-start | bytes 786440 | tf_op jit(solution)/shard_map/ppermute | solution.py:8
  19.4 6.8 %collective-permute-done.2 = f32[256,256]{0,1:T(8,128)S(1)} collective-permute-done((f32[256,256]{0,1:T(8,128)S(1)}, f32[256,256]{0,1:T(8,128)S(1)}, u32[]{:S(2)}, u32[]{:S(2)}) %collective-permute-start.2) | collective-permute-done | bytes 262176 | tf_op jit(solution)/shard_map/ppermute | solution.py:8
  28.2 4.9 %collective-permute-done.3 = f32[256,256]{0,1:T(8,128)S(1)} collective-permute-done((f32[256,256]{0,1:T(8,128)S(1)}, f32[256,256]{0,1:T(8,128)S(1)}, u32[]{:S(2)}, u32[]{:S(2)}) %collective-permute-start.3) | collective-permute-done | bytes 262176 | tf_op jit(solution)/shard_map/ppermute | solution.py:8
  33.1 3.4 %collective-permute-start.4 = (f32[256,256]{0,1:T(8,128)S(1)}, f32[256,256]{0,1:T(8,128)S(1)}, u32[]{:S(2)}, u32[]{:S(2)}) collective-permute-start(f32[256,256]{0,1:T(8,128)S(1)} %add.52), channel_id=1, source_target_pairs={{0,64},{4,68},{8,72},{12,76},{16,80},{20,84},{24,88},{28,92},{32,9... | collective-permute-start | bytes 786440 | tf_op jit(solution)/shard_map/ppermute | solution.py:8
  36.4 9.7 %collective-permute-done.4 = f32[256,256]{0,1:T(8,128)S(1)} collective-permute-done((f32[256,256]{0,1:T(8,128)S(1)}, f32[256,256]{0,1:T(8,128)S(1)}, u32[]{:S(2)}, u32[]{:S(2)}) %collective-permute-start.4) | collective-permute-done | bytes 262176 | tf_op jit(solution)/shard_map/ppermute | solution.py:8
  46.2 6.3 %collective-permute-start.5 = (f32[256,256]{0,1:T(8,128)S(1)}, f32[256,256]{0,1:T(8,128)S(1)}, u32[]{:S(2)}, u32[]{:S(2)}) collective-permute-start(f32[256,256]{0,1:T(8,128)S(1)} %add.53), channel_id=1, source_target_pairs={{0,128},{4,132},{8,136},{12,140},{16,144},{20,148},{24,152},{28,15... | collective-permute-start | bytes 786440 | tf_op jit(solution)/shard_map/ppermute | solution.py:8
  52.5 11.5 %collective-permute-done.5 = f32[256,256]{0,1:T(8,128)S(1)} collective-permute-done((f32[256,256]{0,1:T(8,128)S(1)}, f32[256,256]{0,1:T(8,128)S(1)}, u32[]{:S(2)}, u32[]{:S(2)}) %collective-permute-start.5) | collective-permute-done | bytes 262176 | tf_op jit(solution)/shard_map/ppermute | solution.py:8
  65.7 4.8 %collective-permute-done.6 = f32[256,256]{0,1:T(8,128)S(1)} collective-permute-done((f32[256,256]{0,1:T(8,128)S(1)}, f32[256,256]{0,1:T(8,128)S(1)}, u32[]{:S(2)}, u32[]{:S(2)}) %collective-permute-start.6) | collective-permute-done | bytes 262176 | tf_op jit(solution)/shard_map/ppermute | solution.py:8
  71.3 4.6 %collective-permute-start.7 = (f32[256,256]{0,1:T(8,128)}, f32[256,256]{0,1:T(8,128)}, u32[]{:S(2)}, u32[]{:S(2)}) collective-permute-start(f32[256,256]{0,1:T(8,128)} %add.55), channel_id=1, source_target_pairs={{0,2},{1,3},{2,0},{3,1},{4,6},{5,7},{6,4},{7,5},{8,10},{9,11},{10,... | collective-permute-start | bytes 786440 | tf_op jit(solution)/shard_map/ppermute | solution.py:8
  78.3 2.2 collective-permute-done.7
  85.8 11.7 %cholesky.50 = f32[128,128]{1,0:T(8,128)S(1)} custom-call(f32[128,128]{1,0:T(8,128)S(1)} %cholesky.118), custom_call_target="Cholesky" | custom-call | tf_op jit(solution)/shard_map/jit(cholesky)/cholesky | solution.py:13
  97.6 10.4 %custom-call.15 = f32[1,128,128]{1,2,0:T(8,128)} custom-call(f32[1,128,128]{2,1,0:T(8,128)S(1)} %get-tuple-element.23), custom_call_target="InvertDiagBlocksLowerTriangular" | custom-call | tf_op jit(solution)/shard_map/jit(cholesky)/cholesky | solution.py:13
  111.5 11.7 %cholesky.105 = f32[128,128]{1,0:T(8,128)S(1)} custom-call(f32[128,128]{1,0:T(8,128)S(1)} %slice_subtract_fusion), custom_call_target="Cholesky" | custom-call | tf_op jit(solution)/shard_map/jit(cholesky)/cholesky | solution.py:13
  127.6 7.0 %while.1 = (s32[]{:T(128)}, f32[256,256]{1,0:T(8,128)}, s32[2,2]{1,0:T(2,128)S(1)}, f32[2,128,128]{2,1,0:T(8,128)}, s32[]{:T(128)}) while((s32[]{:T(128)}, f32[256,256]{1,0:T(8,128)}, s32[2,2]{1,0:T(2,128)S(1)}, f32[2,128,128]{2,1,0:T(8,128)}, s32[]{:T(128)}) %tuple.27), condition=%wide.while_cond, body=%wide.while_body.sunk | while | flops 2 | bytes 132205 | solution.py:15
  128.2 2.9 %bitcast_dynamic-update-slice_fusion.2 = f32[2,128,128]{2,1,0:T(8,128)} fusion(f32[2,128,128]{2,1,0:T(8,128)} %get-tuple-element.65, s32[]{:T(128)S(6)} %copy.12, f32[256,256]{1,0:T(8,128)} %get-tuple-element.68, s32[]{:T(128)} %bitcast.38, s32[]{:T(128)} %bitcast.39), kind=kLoop, calls=%fused_computation.clone.1 | loop fusion | bytes 132100 | tf_op jit(solution)/shard_map/jit(_solve_triangular)/triangular_solve
  131.8 2.8 %bitcast_dynamic-update-slice_fusion.2 = f32[2,128,128]{2,1,0:T(8,128)} fusion(f32[2,128,128]{2,1,0:T(8,128)} %get-tuple-element.65, s32[]{:T(128)S(6)} %copy.12, f32[256,256]{1,0:T(8,128)} %get-tuple-element.68, s32[]{:T(128)} %bitcast.38, s32[]{:T(128)} %bitcast.39), kind=kLoop, calls=%fused_computation.clone.1 | loop fusion | bytes 132100 | tf_op jit(solution)/shard_map/jit(_solve_triangular)/triangular_solve
  134.6 21.1 %custom-call.16 = f32[2,128,128]{1,2,0:T(8,128)} custom-call(f32[2,128,128]{2,1,0:T(8,128)} %get-tuple-element.9), custom_call_target="InvertDiagBlocksLowerTriangular" | custom-call | tf_op jit(solution)/shard_map/jit(_solve_triangular)/triangular_solve | solution.py:15
  159.0 3.8 %convolution_multiply_fusion = f32[1536,256]{1,0:T(8,128)} fusion(f32[256,1536]{1,0:T(8,128)S(1)} %fusion.12, f32[128,256]{1,0:T(8,128)S(1)} %fusion.2, f32[128,256]{1,0:T(8,128)S(1)} %fusion.5), kind=kOutput, calls=%fused_computation.2 | convolution fusion | flops 1208418304 | bytes 3407872 | tf_op jit(solution)/shard_map/dot_general | solution.py:42
  162.8 7.6 %all-to-all-start = ((f32[64,24,256]{2,1,0:T(8,128)}), f32[64,24,256]{2,1,0:T(8,128)S(1)}, u32[]{:S(2)}, u32[]{:S(2)}) async-start(f32[64,24,256]{2,1,0:T(8,128)} %bitcast.40), calls=%async_computation | async-start | bytes 3145728 | tf_op jit(solution)/shard_map/all_to_all | solution.py:45
  170.4 3.2 %fusion.1 = f32[2048,256]{1,0:T(8,128)} fusion(bf16[2048,256]{1,0:T(8,128)(2,1)S(1)} %convolution_convert_fusion, f32[128,256]{1,0:T(8,128)S(1)} %fusion.2, f32[128,256]{1,0:T(8,128)} %copy-done.2), kind=kOutput, calls=%fused_computation.12 | convolution fusion | flops 1610678272 | bytes 3407872 | tf_op jit(solution)/shard_map/dot_general | solution.py:38
  173.6 36.8 %all-to-all-done = f32[64,24,256]{2,1,0:T(8,128)S(1)} async-done(((f32[64,24,256]{2,1,0:T(8,128)}), f32[64,24,256]{2,1,0:T(8,128)S(1)}, u32[]{:S(2)}, u32[]{:S(2)}) %all-to-all-start) | async-done | bytes 1572896 | tf_op jit(solution)/shard_map/all_to_all | solution.py:45
  210.6 17.9 %psum.7 = f32[24,256]{1,0:T(8,128)} all-reduce(f32[24,256]{1,0:T(8,128)S(1)} %reduce_sum.9), channel_id=1, replica_groups=mesh['wide'=64,'narrow'=4] {'narrow'}, use_global_device_ids=true, to_apply=%region_5.6 | all-reduce | flops 6144 | bytes 49152 | tf_op jit(solution)/shard_map/psum | solution.py:52
  (45 shorter events, 28.3 us)
Async XLA Ops:
  0.6 1.1 copy-start
  6.4 69.5 %copy-start.1 = (bf16[2048,1536]{1,0:T(8,128)(2,1)S(1)}, bf16[2048,1536]{1,0:T(8,128)(2,1)}, u32[]{:S(2)}) copy-start(bf16[2048,1536]{1,0:T(8,128)(2,1)} %param.2) | copy-start | bytes 18874372
  6.9 1.6 collective-permute-start
  8.6 8.4 %collective-permute-start.1 = (f32[256,256]{0,1:T(8,128)S(1)}, f32[256,256]{0,1:T(8,128)S(1)}, u32[]{:S(2)}, u32[]{:S(2)}) collective-permute-start(f32[256,256]{0,1:T(8,128)S(1)} %add.49), channel_id=1, source_target_pairs={{0,8},{4,12},{8,0},{12,4},{16,24},{20,28},{24,16},{28,20},{32,40},... | collective-permute-start | bytes 786440 | tf_op jit(solution)/shard_map/ppermute | solution.py:8
  17.0 9.1 %collective-permute-start.2 = (f32[256,256]{0,1:T(8,128)S(1)}, f32[256,256]{0,1:T(8,128)S(1)}, u32[]{:S(2)}, u32[]{:S(2)}) collective-permute-start(f32[256,256]{0,1:T(8,128)S(1)} %add.50), channel_id=1, source_target_pairs={{0,16},{4,20},{8,24},{12,28},{16,0},{20,4},{24,8},{28,12},{32,48},... | collective-permute-start | bytes 786440 | tf_op jit(solution)/shard_map/ppermute | solution.py:8
  26.2 6.9 %collective-permute-start.3 = (f32[256,256]{0,1:T(8,128)S(1)}, f32[256,256]{0,1:T(8,128)S(1)}, u32[]{:S(2)}, u32[]{:S(2)}) collective-permute-start(f32[256,256]{0,1:T(8,128)S(1)} %add.51), channel_id=1, source_target_pairs={{0,32},{4,36},{8,40},{12,44},{16,48},{20,52},{24,56},{28,60},{32,0... | collective-permute-start | bytes 786440 | tf_op jit(solution)/shard_map/ppermute | solution.py:8
  33.1 13.1 %collective-permute-start.4 = (f32[256,256]{0,1:T(8,128)S(1)}, f32[256,256]{0,1:T(8,128)S(1)}, u32[]{:S(2)}, u32[]{:S(2)}) collective-permute-start(f32[256,256]{0,1:T(8,128)S(1)} %add.52), channel_id=1, source_target_pairs={{0,64},{4,68},{8,72},{12,76},{16,80},{20,84},{24,88},{28,92},{32,9... | collective-permute-start | bytes 786440 | tf_op jit(solution)/shard_map/ppermute | solution.py:8
  46.2 17.8 %collective-permute-start.5 = (f32[256,256]{0,1:T(8,128)S(1)}, f32[256,256]{0,1:T(8,128)S(1)}, u32[]{:S(2)}, u32[]{:S(2)}) collective-permute-start(f32[256,256]{0,1:T(8,128)S(1)} %add.53), channel_id=1, source_target_pairs={{0,128},{4,132},{8,136},{12,140},{16,144},{20,148},{24,152},{28,15... | collective-permute-start | bytes 786440 | tf_op jit(solution)/shard_map/ppermute | solution.py:8
  64.1 6.5 %collective-permute-start.6 = (f32[256,256]{0,1:T(8,128)S(1)}, f32[256,256]{0,1:T(8,128)S(1)}, u32[]{:S(2)}, u32[]{:S(2)}) collective-permute-start(f32[256,256]{0,1:T(8,128)S(1)} %add.54), channel_id=1, source_target_pairs={{0,1},{1,0},{2,3},{3,2},{4,5},{5,4},{6,7},{7,6},{8,9},{9,8},{10,11... | collective-permute-start | bytes 786440 | tf_op jit(solution)/shard_map/ppermute | solution.py:8
  71.3 9.3 %collective-permute-start.7 = (f32[256,256]{0,1:T(8,128)}, f32[256,256]{0,1:T(8,128)}, u32[]{:S(2)}, u32[]{:S(2)}) collective-permute-start(f32[256,256]{0,1:T(8,128)} %add.55), channel_id=1, source_target_pairs={{0,2},{1,3},{2,0},{3,1},{4,6},{5,7},{6,4},{7,5},{8,10},{9,11},{10,... | collective-permute-start | bytes 786440 | tf_op jit(solution)/shard_map/ppermute | solution.py:8
  85.1 0.7 copy-start.3
  159.0 3.8 %copy-start.2 = (f32[128,256]{1,0:T(8,128)}, f32[128,256]{1,0:T(8,128)S(1)}, u32[]{:S(2)}) copy-start(f32[128,256]{1,0:T(8,128)S(1)} %fusion.5) | copy-start | bytes 393220
  162.8 47.6 %all-to-all-start = ((f32[64,24,256]{2,1,0:T(8,128)}), f32[64,24,256]{2,1,0:T(8,128)S(1)}, u32[]{:S(2)}, u32[]{:S(2)}) async-start(f32[64,24,256]{2,1,0:T(8,128)} %bitcast.40), calls=%async_computation | async-start | bytes 3145728 | tf_op jit(solution)/shard_map/all_to_all | solution.py:45
where the time goes:
time: 229 us
  waiting for transfers between devices  85.4 us (37%)
  other arithmetic  62.6 us (27%)
  starting transfers between devices  29.2 us (13%)
  matrix products  20 us (9%)
  blocking collectives  17.9 us (8%)
  local copies, waits for them, and re-layouts  11.4 us (5%)
    ppermute x8, waiting for transfers between devices, from_partner(): lax.ppermute(x, axis, [(i, i ^ 1 << bit) for i in range(lax.axis_size(axi...  48.5 us
    all_to_all x1, waiting for transfers between devices, body(): lax.all_to_all(cross_terms.reshape(n_wide, owned_cols, rank_cols), 'wide'...  36.8 us
    another operation x6, other arithmetic, factor_inverse(): lower = jnp.linalg.cholesky(gram)  35.2 us
    another operation x3, other arithmetic, factor_inverse(): jax.scipy.linalg.solve_triangular(lower, identity, trans='T', lower=True)  22.8 us
    ppermute x8, starting transfers between devices, from_partner(): lax.ppermute(x, axis, [(i, i ^ 1 << bit) for i in range(lax.axis_size(axi...  21.6 us
    psum x1, blocking collectives, body(): owned_rows = lax.psum(jnp.sum(pieces, axis=0), 'narrow')  17.9 us
    all_to_all x1, starting transfers between devices, body(): lax.all_to_all(cross_terms.reshape(n_wide, owned_cols, rank_cols), 'wide'...  7.6 us
    another operation x6, local copies, waits for them, and re-layouts  6.98 us
  transfers between devices with their start and end apart: 9, of which 9 were waited for; matrix products, arithmetic and copies ran while one was open for 2% of the time, Pallas kernels for 0%

commit v1 on v0

v1 whole, which is shorter than its diff:
```python
import functools

import jax
import jax.numpy as jnp
from jax import lax
from jax.experimental import pallas as pl
from jax.experimental.pallas import tpu as pltpu
from jax.sharding import PartitionSpec as P

LANES = 128
SUB = 8
CHUNK = 256


def barrier(*values):
    return lax.optimization_barrier(values)


def shifted(x, axis, target):
    return lax.ppermute(x, axis, [(i, target(i)) for i in range(lax.axis_size(axis))])


def along_z(target):
    return lambda i: (target(i >> 3) % 8) << 3 | i & 7


Z_PAIR = along_z(lambda z: z ^ 1)
Z_NEXT = along_z(lambda z: z + 1 if z % 2 else z - 1)
Z_TWO = along_z(lambda z: z + 2 if z % 2 else z - 2)
Z_THREE = along_z(lambda z: z + 3 if z % 2 else z - 3)


def along_x(bits):
    return lambda i: i ^ bits << 1


def other_core(i):
    return i ^ 1


def flip(bits):
    return lambda i: i ^ bits


def sum4(parts):
    return (parts[0] + parts[1]) + (parts[2] + parts[3])


def splat(x, sub=None, lane=None):
    if lane is not None:
        x = x[:, lane : lane + 1]
    if sub is not None:
        x = x[sub : sub + 1, :]
    return jnp.broadcast_to(x, (SUB, LANES))


def factor_in_place(s, order):
    halves = order // LANES
    row = lax.broadcasted_iota(jnp.int32, (SUB, LANES), 0)
    lane = lax.broadcasted_iota(jnp.int32, (SUB, LANES), 1)

    def tile(r, h):
        return (slice(r, r + SUB), slice(LANES * h, LANES * (h + 1)))

    for p0 in range(0, order, LANES):
        p1 = p0 + LANES
        here = p0 // LANES
        for r0 in range(p0, p1, SUB):
            l0 = r0 - p0
            last = r0 + SUB >= p1
            fwd = [s[tile(r0, h)] for h in range(halves)]
            cols = [splat(fwd[here], lane=l0 + k) for k in range(SUB)]
            pivots = (lane >= l0) & (lane < l0 + SUB)
            fwd[here] = jnp.where(pivots, jnp.where(lane - l0 == row, 1.0, 0.0), fwd[here])
            both = list(fwd)
            inv_d = jnp.zeros((SUB, LANES), jnp.float32)
            for i in range(SUB):
                recip = 1.0 / splat(cols[i], sub=i)
                mult = cols[i] * recip
                below = jnp.where(row > i, mult, 0.0)
                others = jnp.where(row != i, mult, 0.0)
                inv_d = jnp.where(row == i, recip, inv_d)
                for k in range(i + 1, SUB):
                    cols[k] = cols[k] - (below if last else others) * splat(cols[k], sub=i)
                for h in range(halves):
                    pivot_row = splat(fwd[h], sub=i)
                    fwd[h] = fwd[h] - below * pivot_row
                    if not last:
                        both[h] = both[h] - others * pivot_row
            if not last:
                both = [b * inv_d for b in both]
                rows = [[splat(b, sub=k) for b in both] for k in range(SUB)]
                for g0 in range(r0 + SUB, p1, SUB):
                    old = [s[tile(g0, h)] for h in range(halves)]
                    coef = [splat(old[here], lane=l0 + k) for k in range(SUB)]
                    old[here] = jnp.where(pivots, 0.0, old[here])
                    for h in range(halves):
                        t = [coef[k] * rows[k][h] for k in range(SUB)]
                        s[tile(g0, h)] = old[h] - (sum4(t[:4]) + sum4(t[4:]))
            scale = jnp.sqrt(inv_d)
            for h in range(halves):
                s[tile(r0, h)] = fwd[h] * scale
        if p1 < order:
            panel = s[p0:p1, :]
            r = lax.broadcasted_iota(jnp.int32, panel.shape, 0)
            c = lax.broadcasted_iota(jnp.int32, panel.shape, 1)
            panel = jnp.where((c < p1) & (c > p0 + r), 0.0, panel)
            update = lax.dot_general(
                panel[:, p1:],
                panel,
                (((0,), (0,)), ((), ())),
                precision=lax.Precision.HIGHEST,
                preferred_element_type=jnp.float32,
            )
            c = lax.broadcasted_iota(jnp.int32, update.shape, 1)
            s[p1:, :] = jnp.where((c >= p0) & (c < p1), 0.0, s[p1:, :]) - update


def basis_kernel(core, mine, other, sketch, inv_t, basis, s, out, sems):
    first = core[0] == 0
    half = mine.shape[0]
    a, b = mine[...], other[...]
    low = jnp.where(first, a, b)
    high = jnp.where(first, b, a)
    s[:LANES, :LANES] = low[:LANES]
    s[: half - LANES, LANES:] = low[LANES:]
    s[half - LANES : LANES, LANES:] = high[: 2 * LANES - half]
    s[LANES:, LANES:] = high[2 * LANES - half :]
    order = s.shape[0]
    factor_in_place(s, order)
    r = lax.broadcasted_iota(jnp.int32, s.shape, 0)
    c = lax.broadcasted_iota(jnp.int32, s.shape, 1)
    inv = jnp.where(c <= r, s[...], 0.0)
    inv_t[...] = inv
    hi = inv.astype(jnp.bfloat16)
    rest = inv - hi.astype(jnp.float32)
    mid = rest.astype(jnp.bfloat16)
    low = (rest - mid.astype(jnp.float32)).astype(jnp.bfloat16)
    copies = []
    for n in range(sketch.shape[0] // CHUNK):
        rows = slice(n * CHUNK, (n + 1) * CHUNK)
        x = sketch[rows, :]
        total = None
        for part in (low, mid, hi):
            term = lax.dot_general(
                x, part, (((1,), (1,)), ((), ())), preferred_element_type=jnp.float32
            )
            total = term if total is None else total + term
        out[rows, :] = total
        copy = pltpu.make_async_copy(out.at[rows, :], basis.at[rows, :], sems.at[n])
        copy.start()
        copies.append(copy)
    for copy in copies:
        copy.wait()


def finish(core, mine, other, sketch):
    rows, order = sketch.shape
    vmem = pl.BlockSpec(memory_space=pltpu.VMEM)
    return pl.pallas_call(
        basis_kernel,
        out_shape=(
            jax.ShapeDtypeStruct((order, order), jnp.float32),
            jax.ShapeDtypeStruct((rows, order), jnp.float32),
        ),
        in_specs=[pl.BlockSpec(memory_space=pltpu.SMEM), vmem, vmem, vmem],
        out_specs=(vmem, pl.BlockSpec(memory_space=pl.ANY)),
        scratch_shapes=[
            pltpu.VMEM((order, order), jnp.float32),
            pltpu.VMEM((rows, order), jnp.float32),
            pltpu.SemaphoreType.DMA((rows // CHUNK,)),
        ],
        compiler_params=pltpu.CompilerParams(vmem_limit_bytes=24 * 2**20),
    )(core, mine, other, sketch)


def pick(x, index):
    return lax.dynamic_index_in_dim(x, index, 0, keepdims=False)


def body(embeddings, test_matrix):
    n_wide = lax.axis_size("wide")
    rows_total = embeddings.shape[0] * n_wide * lax.axis_size("narrow")
    place = lax.axis_index("wide")
    core, x_at, z_at = place & 1, place >> 1 & 3, place >> 3
    sketch = jnp.dot(embeddings, test_matrix, preferred_element_type=jnp.float32).astype(
        jnp.bfloat16
    )
    gram = (
        lax.dot_general(
            sketch, sketch, (((0,), (0,)), ((), ())), preferred_element_type=jnp.float32
        )
        / rows_total
    )
    packed = jnp.concatenate([gram[:LANES, :LANES], gram[:LANES, LANES:], gram[LANES:, LANES:]])
    top, bottom = jnp.split(packed, 2)
    mine = jnp.where(core == 0, top, bottom)
    theirs = jnp.where(core == 0, bottom, top)
    mine = mine + shifted(theirs, "wide", other_core)

    cross = lax.dot_general(
        embeddings, sketch, (((0,), (0,)), ((), ())), preferred_element_type=jnp.float32
    )
    owned = cross.shape[0] // n_wide
    cross = cross.reshape(8, 4, 2, owned, cross.shape[1])
    kept = jnp.where(core == 0, cross[:, :, 0], cross[:, :, 1])
    given = jnp.where(core == 0, cross[:, :, 1], cross[:, :, 0])
    mine, kept, given = barrier(mine, kept, given)

    mine = mine + shifted(mine, "wide", Z_PAIR)
    kept = (kept + shifted(given, "wide", other_core)).transpose(1, 0, 2, 3)
    mine, kept = barrier(mine, kept)

    if CROSS == "a2a":
        groups_x = [[z * 8 + x * 2 + c for x in range(4)] for z in range(8) for c in range(2)]
        groups_z = [[z * 8 + r for z in range(8)] for r in range(8)]
        kx = lax.all_to_all(kept, "wide", 0, 0, tiled=True, axis_index_groups=groups_x)
        mine = sum4([mine] + [shifted(mine, "wide", t) for t in (Z_NEXT, Z_TWO, Z_THREE)])
        mine, = barrier(mine)
        mine = sum4([mine] + [shifted(mine, "narrow", flip(k)) for k in (1, 2, 3)])
        mine, kept = barrier(mine, kx)
        kept = jnp.sum(kept, axis=0)
        kz = lax.all_to_all(kept, "wide", 0, 0, tiled=True, axis_index_groups=groups_z)
        mine = sum4([mine] + [shifted(mine, "wide", along_x(k)) for k in (1, 2, 3)])
        mine, = barrier(mine)
        other = shifted(mine, "wide", other_core)
        other, kept = barrier(other, kz)
        kept = jnp.sum(kept, axis=0)
    else:
        parts = [pick(kept, x_at ^ k) for k in range(4)]
        mine = sum4([mine] + [shifted(mine, "wide", t) for t in (Z_NEXT, Z_TWO, Z_THREE)])
        kept = sum4(parts[:1] + [shifted(parts[k], "wide", along_x(k)) for k in (1, 2, 3)])
        mine, kept = barrier(mine, kept)
        kept = kept.reshape(4, 2, owned, -1)
        parts = [pick(kept, (z_at >> 1) ^ k) for k in range(4)]
        mine = sum4([mine] + [shifted(mine, "narrow", flip(k)) for k in (1, 2, 3)])
        kept = sum4(
            parts[:1]
            + [shifted(parts[k], "wide", along_z(lambda z, k=k: z ^ 2 * k)) for k in (1, 2, 3)]
        )
        mine, kept = barrier(mine, kept)
        parts = [pick(kept, (z_at & 1) ^ k) for k in range(2)]
        mine = sum4([mine] + [shifted(mine, "wide", along_x(k)) for k in (1, 2, 3)])
        kept = parts[0] + shifted(parts[1], "wide", Z_PAIR)
        mine, kept = barrier(mine, kept)
        other = shifted(mine, "wide", other_core)
    kept = sum4([kept] + [shifted(kept, "narrow", flip(k)) for k in (1, 2, 3)])
    inv_t, basis_rows = finish(core.reshape(1), mine, other, sketch)
    loadings = (
        lax.dot_general(
            kept, inv_t, (((1,), (1,)), ((), ())), precision=lax.Precision.HIGHEST
        )
        / rows_total
    )
    return (basis_rows, loadings)


CROSS = "a2a"


def solution(mesh):
    in_specs = (P(("wide", "narrow"), None), P())
    out_specs = (P(("wide", "narrow"), None), P("wide", None))
    return jax.shard_map(body, mesh=mesh, in_specs=in_specs, out_specs=out_specs, check_vma=False)
```

time: 229 us -> 84.5 us (0.37)
  waiting for transfers between devices: 85.4 us -> 17.7 us
  other arithmetic: 62.6 us -> 2.82 us
  blocking collectives: 17.9 us -> 0 us
  Pallas kernels: 0 us -> 11.8 us
  matrix products: 20 us -> 11.7 us
  local copies, waits for them, and re-layouts: 11.4 us -> 3.98 us
  starting transfers between devices: 29.2 us -> 35.1 us
    another operation x9 -> x0, other arithmetic: 58 us -> none  [the longest x6 35.2 us: factor_inverse(): lower = jnp.linalg.cholesky(gram)]
    ppermute x8 -> x16, waiting for transfers between devices: 48.5 us -> 9.41 us  [shifted(): lax.ppermute(x, axis, [(i, target(i)) for i in range(lax.axis_size(axis))])]
    all_to_all x1 -> x2, waiting for transfers between devices: 36.8 us -> 8.34 us  [the longest x1 8.33 us: body(): lax.all_to_all(kept, 'wide', 0, 0, tiled=True, axis_index_groups=groups_z)]
    psum x1 -> x0, blocking collectives: 17.9 us -> none  [body(): owned_rows = lax.psum(jnp.sum(pieces, axis=0), 'narrow')]
    pallas_call x0 -> x1, Pallas kernels: none -> 11.8 us  [finish(): pl.pallas_call(basis_kernel, out_shape=(jax.ShapeDtypeStruct((order, orde...]
    another operation x9 -> x0, local copies, waits for them, and re-layouts: 7.76 us -> none
    dot_general x2 -> x1, matrix products: 7.03 us -> 0.94 us  [body(): lax.dot_general(kept, inv_t, (((1,), (1,)), ((), ())), precision=lax.Prec...]
    another operation x5 -> x0, matrix products: 6.09 us -> none  [the longest x3 3.3 us: factor_inverse(): jax.scipy.linalg.solve_triangular(lower, identity, trans='T', lower=True)]
  transfers between devices with their start and end apart: 9 -> 18, of which waited for: 9 -> 5; matrix products, arithmetic and copies ran while one was open for 2% -> 11% of each run, Pallas kernels for 0% -> 14%
where the time goes in v1:
time: 84.5 us; the launch traced here: 84.1 us
  starting transfers between devices  35.1 us (42%)
  waiting for transfers between devices  17.7 us (21%)
  Pallas kernels  11.8 us (14%)
  matrix products  11.7 us (14%)
  local copies, waits for them, and re-layouts  3.98 us (5%)
  other arithmetic  2.82 us (3%)
  between operations  0.86 us (1%)
    ppermute x16, starting transfers between devices, shifted(): lax.ppermute(x, axis, [(i, target(i)) for i in range(lax.axis_size(axis))])  25.7 us
    pallas_call x1, Pallas kernels, finish(): pl.pallas_call(basis_kernel, out_shape=(jax.ShapeDtypeStruct((order, orde...  11.8 us
    ppermute x16, waiting for transfers between devices, shifted(): lax.ppermute(x, axis, [(i, target(i)) for i in range(lax.axis_size(axis))])  9.41 us
    all_to_all x1, waiting for transfers between devices, body(): lax.all_to_all(kept, 'wide', 0, 0, tiled=True, axis_index_groups=groups_z)  8.33 us
    dot_general x1, matrix products, body(): lax.dot_general(embeddings, sketch, (((0,), (0,)), ((), ())), preferred_e...  5.73 us
    all_to_all x1, starting transfers between devices, body(): lax.all_to_all(kept, 'wide', 0, 0, tiled=True, axis_index_groups=groups_x)  4.8 us
    all_to_all x1, starting transfers between devices, body(): lax.all_to_all(kept, 'wide', 0, 0, tiled=True, axis_index_groups=groups_z)  4.68 us
    dot_general x1, matrix products, body(): jnp.dot(embeddings, test_matrix, preferred_element_type=jnp.float32)  4.58 us
  transfers between devices with their start and end apart: 18, of which 5 were waited for; matrix products, arithmetic and copies ran while one was open for 11% of the time, Pallas kernels for 14%

profile of v1, /device:TPU:4, one launch (start us, length us, event | category | flops | bytes accessed | tf_op | source)
XLA Modules:
  0.0 84.1 jit_solution(11366966373287859099)
XLA Ops:
  0.6 1.1 %copy-done = bf16[1536,256]{1,0:T(8,128)(2,1)S(1)} copy-done((bf16[1536,256]{1,0:T(8,128)(2,1)S(1)}, bf16[1536,256]{1,0:T(8,128)(2,1)}, u32[]{:S(2)}) %copy-start) | copy-done | bytes 786456
  1.8 4.6 %convolution_convert_fusion.sketch = bf16[2048,256]{1,0:T(8,128)(2,1)S(1)} fusion(bf16[2048,1536]{1,0:T(8,128)(2,1)} %param.2, bf16[1536,256]{1,0:T(8,128)(2,1)S(1)} %copy-done), kind=kOutput, calls=%fused_computation.1 | convolution fusion | flops 1611137024 | bytes 8126464 | tf_op jit(solution)/shard_map/dot_general | solution.py:186
  7.6 5.7 %convolution_bitcast_fusion = f32[1536,256]{0,1:T(8,128)} fusion(bf16[2048,256]{1,0:T(8,128)(2,1)S(1)} %convolution_convert_fusion.sketch, bf16[2048,1536]{1,0:T(8,128)(2,1)} %param.2), kind=kOutput, calls=%fused_computation | convolution fusion | flops 1610612736 | bytes 8912896 | tf_op jit(solution)/shard_map/dot_general | solution.py:201
  13.3 1.9 %copy.13 = f32[1536,256]{1,0:T(8,128)S(1)} copy(f32[1536,256]{0,1:T(8,128)} %convolution_bitcast_fusion) | data formatting | bytes 3145728 | tf_op jit(solution)/shard_map/dot_general | solution.py:201
  15.5 1.0 %select_add_fusion = f32[192,128]{1,0:T(8,128)S(1)} fusion(f32[192,128]{1,0:T(8,128)} %collective-permute-done, f32[256,256]{1,0:T(8,128)} %copy-done.1, pred[]{:T(512)S(6)} %eq.2, f32[256,128]{1,0:T(8,128)S(1)} %slice.23, f32[128,128]{1,0:T(8,128)} %copy-done.2), kind=kLoop, calls=%fused_computation.12 | loop fusion | flops 73728 | bytes 491521 | tf_op jit(solution)/shard_map/add | solution.py:199
  17.0 1.9 %collective-permute-start.1 = (f32[192,128]{1,0:T(8,128)S(1)}, f32[192,128]{1,0:T(8,128)S(1)}, u32[]{:S(2)}, u32[]{:S(2)}) collective-permute-start(f32[192,128]{1,0:T(8,128)S(1)} %select_add_fusion), channel_id=1, source_target_pairs={{0,32},{4,36},{8,40},{12,44},{16,48},{20,52},{24,56},{28,60},{32,0... | collective-permute-start | bytes 294920 | tf_op jit(solution)/shard_map/ppermute | solution.py:20
  19.0 3.1 %collective-permute-done.1 = f32[192,128]{1,0:T(8,128)S(1)} collective-permute-done((f32[192,128]{1,0:T(8,128)S(1)}, f32[192,128]{1,0:T(8,128)S(1)}, u32[]{:S(2)}, u32[]{:S(2)}) %collective-permute-start.1) | collective-permute-done | bytes 98336 | tf_op jit(solution)/shard_map/ppermute | solution.py:20
  22.2 6.7 %collective-permute-start.5 = (f32[192,128]{1,0:T(8,128)S(1)}, f32[192,128]{1,0:T(8,128)S(1)}, u32[]{:S(2)}, u32[]{:S(2)}) collective-permute-start(f32[192,128]{1,0:T(8,128)S(1)} %add.46), channel_id=1, source_target_pairs={{0,160},{4,164},{8,168},{12,172},{16,176},{20,180},{24,184},{28,18... | collective-permute-start | bytes 294920 | tf_op jit(solution)/shard_map/ppermute | solution.py:20
  29.4 3.1 %collective-permute-start.3 = (f32[192,128]{1,0:T(8,128)S(1)}, f32[192,128]{1,0:T(8,128)S(1)}, u32[]{:S(2)}, u32[]{:S(2)}) collective-permute-start(f32[192,128]{1,0:T(8,128)S(1)} %add.46), channel_id=1, source_target_pairs={{0,224},{4,228},{8,232},{12,236},{16,240},{20,244},{24,248},{28,25... | collective-permute-start | bytes 294920 | tf_op jit(solution)/shard_map/ppermute | solution.py:20
  32.5 1.0 %copy.18 = f32[4,8,24,256]{3,2,1,0:T(8,128)} copy(f32[4,8,24,256]{3,2,0,1:T(8,128)S(1)} %add_bitcast_fusion) | data formatting | bytes 1572864 | tf_op jit(solution)/shard_map/optimization_barrier | solution.py:16
  33.4 4.8 %all-to-all-start = ((f32[4,8,24,256]{3,2,1,0:T(8,128)}), f32[4,8,24,256]{3,2,1,0:T(8,128)S(1)}, u32[]{:S(2)}, u32[]{:S(2)}) async-start(f32[4,8,24,256]{3,2,1,0:T(8,128)} %copy.18), calls=%async_computation | async-start | bytes 1572864 | tf_op jit(solution)/shard_map/all_to_all | solution.py:217
  38.3 3.1 %collective-permute-start.8 = (f32[192,128]{1,0:T(8,128)S(1)}, f32[192,128]{1,0:T(8,128)S(1)}, u32[]{:S(2)}, u32[]{:S(2)}) collective-permute-start(f32[192,128]{1,0:T(8,128)S(1)} %add_add_fusion.2), channel_id=1, source_target_pairs={{0,3},{1,2},{2,1},{3,0},{4,7},{5,6},{6,5},{7,4},{8,11},{9,10},{10,... | collective-permute-start | bytes 294920 | tf_op jit(solution)/shard_map/ppermute | solution.py:20
  42.5 2.7 %collective-permute-done.8 = f32[192,128]{1,0:T(8,128)S(1)} collective-permute-done((f32[192,128]{1,0:T(8,128)S(1)}, f32[192,128]{1,0:T(8,128)S(1)}, u32[]{:S(2)}, u32[]{:S(2)}) %collective-permute-start.8) | collective-permute-done | bytes 98336 | tf_op jit(solution)/shard_map/ppermute | solution.py:20
  45.2 2.3 %collective-permute-done.7 = f32[192,128]{1,0:T(8,128)S(1)} collective-permute-done((f32[192,128]{1,0:T(8,128)S(1)}, f32[192,128]{1,0:T(8,128)S(1)}, u32[]{:S(2)}, u32[]{:S(2)}) %collective-permute-start.7) | collective-permute-done | bytes 98336 | tf_op jit(solution)/shard_map/ppermute | solution.py:20
  48.2 2.6 %collective-permute-start.10 = (f32[192,128]{1,0:T(8,128)S(1)}, f32[192,128]{1,0:T(8,128)S(1)}, u32[]{:S(2)}, u32[]{:S(2)}) collective-permute-start(f32[192,128]{1,0:T(8,128)S(1)} %add_add_fusion.1), channel_id=1, source_target_pairs={{0,16},{4,20},{8,24},{12,28},{16,0},{20,4},{24,8},{28,12},{32,48},... | collective-permute-start | bytes 294920 | tf_op jit(solution)/shard_map/ppermute | solution.py:20
  50.9 0.9 %collective-permute-start.9 = (f32[192,128]{1,0:T(8,128)S(1)}, f32[192,128]{1,0:T(8,128)S(1)}, u32[]{:S(2)}, u32[]{:S(2)}) collective-permute-start(f32[192,128]{1,0:T(8,128)S(1)} %add_add_fusion.1), channel_id=1, source_target_pairs={{0,8},{4,12},{8,0},{12,4},{16,24},{20,28},{24,16},{28,20},{32,40},... | collective-permute-start | bytes 294920 | tf_op jit(solution)/shard_map/ppermute | solution.py:20
  51.7 0.7 reduce_sum.18
  52.4 4.7 %all-to-all-start.1 = ((f32[8,24,256]{2,1,0:T(8,128)}), f32[8,24,256]{2,1,0:T(8,128)S(1)}, u32[]{:S(2)}, u32[]{:S(2)}) async-start(f32[8,24,256]{2,1,0:T(8,128)} %reduce_sum.18), calls=%async_computation.1 | async-start | bytes 393216 | tf_op jit(solution)/shard_map/all_to_all | solution.py:223
  57.3 1.3 %collective-permute-done.12.other = f32[192,128]{1,0:T(8,128)S(1)} collective-permute-done((f32[192,128]{1,0:T(8,128)S(1)}, f32[192,128]{1,0:T(8,128)S(1)}, u32[]{:S(2)}, u32[]{:S(2)}) %collective-permute-start.12) | collective-permute-done | bytes 98336 | tf_op jit(solution)/shard_map/ppermute | solution.py:20
  58.6 8.3 %all-to-all-done.1 = f32[8,24,256]{2,1,0:T(8,128)S(1)} async-done(((f32[8,24,256]{2,1,0:T(8,128)}), f32[8,24,256]{2,1,0:T(8,128)S(1)}, u32[]{:S(2)}, u32[]{:S(2)}) %all-to-all-start.1) | async-done | bytes 196640 | tf_op jit(solution)/shard_map/all_to_all | solution.py:223
  66.9 1.9 %collective-permute-start.15 = (f32[24,256]{1,0:T(8,128)S(1)}, f32[24,256]{1,0:T(8,128)S(1)}, u32[]{:S(2)}, u32[]{:S(2)}) collective-permute-start(f32[24,256]{1,0:T(8,128)S(1)} %reduce_sum.19), channel_id=1, source_target_pairs={{0,3},{1,2},{2,1},{3,0},{4,7},{5,6},{6,5},{7,4},{8,11},{9,10},{10,... | collective-permute-start | bytes 73736 | tf_op jit(solution)/shard_map/ppermute | solution.py:20
  69.4 1.9 %collective-permute-start.13 = (f32[24,256]{1,0:T(8,128)S(1)}, f32[24,256]{1,0:T(8,128)S(1)}, u32[]{:S(2)}, u32[]{:S(2)}) collective-permute-start(f32[24,256]{1,0:T(8,128)S(1)} %reduce_sum.19), channel_id=1, source_target_pairs={{0,1},{1,0},{2,3},{3,2},{4,5},{5,4},{6,7},{7,6},{8,9},{9,8},{10,11... | collective-permute-start | bytes 73736 | tf_op jit(solution)/shard_map/ppermute | solution.py:20
  71.3 11.8 %shard_map.41 = (f32[256,256]{1,0:T(8,128)S(1)}, f32[2048,256]{1,0:T(8,128)}) custom-call(s32[1]{0:T(128)} %bitcast.core, f32[192,128]{1,0:T(8,128)S(1)} %add_add_fusion.mine, f32[192,128]{1,0:T(8,128)S(1)} %collective-permute-done.12.other, bf16[2048,256]{1,0:T(8,128)(2,1)S(1)} %convolution_convert_fusion.sketch), custom_call_target="tpu_custom_call" | custom-call | tf_op jit(solution)/shard_map/pallas_call | solution.py:160
  83.1 0.9 %convolution_multiply_fusion.1 = f32[24,256]{1,0:T(8,128)} fusion(f32[256,256]{1,0:T(8,128)S(1)} %get-tuple-element.23, f32[24,256]{1,0:T(8,128)S(1)} %collective-permute-done.14, f32[24,256]{1,0:T(8,128)S(1)} %collective-permute-done.15, f32[24,256]{1,0:T(8,128)S(1)} %reduce_sum.19, f32[24,256]{1,0:T(8,128)S(1)} %collective-permute-done.13), kind=kOutput, calls=%fused_computation.3 | convolution fusion | flops 18898944 | bytes 385024 | tf_op jit(solution)/shard_map/dot_general | solution.py:250
  (38 shorter events, 5.3 us)
Async XLA Ops:
  0.6 1.1 %copy-start = (bf16[1536,256]{1,0:T(8,128)(2,1)S(1)}, bf16[1536,256]{1,0:T(8,128)(2,1)}, u32[]{:S(2)}) copy-start(bf16[1536,256]{1,0:T(8,128)(2,1)} %param.3) | copy-start | bytes 2359300
  6.8 0.8 copy-start.1
  6.9 0.7 copy-start.2
  7.6 7.9 %collective-permute-start = (f32[192,128]{1,0:T(8,128)}, f32[192,128]{1,0:T(8,128)}, u32[]{:S(2)}, u32[]{:S(2)}) collective-permute-start(f32[192,128]{1,0:T(8,128)} %slice_select_fusion), channel_id=1, source_target_pairs={{0,4},{4,0},{8,12},{12,8},{16,20},{20,16},{24,28},{28,24},{32,36},... | collective-permute-start | bytes 294920 | tf_op jit(solution)/shard_map/ppermute | solution.py:20
  16.4 5.6 %collective-permute-start.2 = (f32[8,4,24,256]{3,2,1,0:T(8,128)S(1)}, f32[8,4,24,256]{3,2,1,0:T(8,128)S(1)}, u32[]{:S(2)}, u32[]{:S(2)}) collective-permute-start(f32[8,4,24,256]{3,2,1,0:T(8,128)S(1)} %select_bitcast_fusion), channel_id=1, source_target_pairs={{0,4},{4,0},{8,12},{12,8},{16,20},{20,16},{24,28},{28,24},{32,36},... | collective-permute-start | bytes 2359304 | tf_op jit(solution)/shard_map/ppermute | solution.py:20
  17.0 5.0 %collective-permute-start.1 = (f32[192,128]{1,0:T(8,128)S(1)}, f32[192,128]{1,0:T(8,128)S(1)}, u32[]{:S(2)}, u32[]{:S(2)}) collective-permute-start(f32[192,128]{1,0:T(8,128)S(1)} %select_add_fusion), channel_id=1, source_target_pairs={{0,32},{4,36},{8,40},{12,44},{16,48},{20,52},{24,56},{28,60},{32,0... | collective-permute-start | bytes 294920 | tf_op jit(solution)/shard_map/ppermute | solution.py:20
  22.2 16.1 %collective-permute-start.5 = (f32[192,128]{1,0:T(8,128)S(1)}, f32[192,128]{1,0:T(8,128)S(1)}, u32[]{:S(2)}, u32[]{:S(2)}) collective-permute-start(f32[192,128]{1,0:T(8,128)S(1)} %add.46), channel_id=1, source_target_pairs={{0,160},{4,164},{8,168},{12,172},{16,176},{20,180},{24,184},{28,18... | collective-permute-start | bytes 294920 | tf_op jit(solution)/shard_map/ppermute | solution.py:20
  28.8 9.4 %collective-permute-start.4 = (f32[192,128]{1,0:T(8,128)S(1)}, f32[192,128]{1,0:T(8,128)S(1)}, u32[]{:S(2)}, u32[]{:S(2)}) collective-permute-start(f32[192,128]{1,0:T(8,128)S(1)} %add.46), channel_id=1, source_target_pairs={{0,192},{4,196},{8,200},{12,204},{16,208},{20,212},{24,216},{28,22... | collective-permute-start | bytes 294920 | tf_op jit(solution)/shard_map/ppermute | solution.py:20
  29.4 8.9 %collective-permute-start.3 = (f32[192,128]{1,0:T(8,128)S(1)}, f32[192,128]{1,0:T(8,128)S(1)}, u32[]{:S(2)}, u32[]{:S(2)}) collective-permute-start(f32[192,128]{1,0:T(8,128)S(1)} %add.46), channel_id=1, source_target_pairs={{0,224},{4,228},{8,232},{12,236},{16,240},{20,244},{24,248},{28,25... | collective-permute-start | bytes 294920 | tf_op jit(solution)/shard_map/ppermute | solution.py:20
  33.4 14.1 %all-to-all-start = ((f32[4,8,24,256]{3,2,1,0:T(8,128)}), f32[4,8,24,256]{3,2,1,0:T(8,128)S(1)}, u32[]{:S(2)}, u32[]{:S(2)}) async-start(f32[4,8,24,256]{3,2,1,0:T(8,128)} %copy.18), calls=%async_computation | async-start | bytes 1572864 | tf_op jit(solution)/shard_map/all_to_all | solution.py:217
  38.3 6.9 %collective-permute-start.8 = (f32[192,128]{1,0:T(8,128)S(1)}, f32[192,128]{1,0:T(8,128)S(1)}, u32[]{:S(2)}, u32[]{:S(2)}) collective-permute-start(f32[192,128]{1,0:T(8,128)S(1)} %add_add_fusion.2), channel_id=1, source_target_pairs={{0,3},{1,2},{2,1},{3,0},{4,7},{5,6},{6,5},{7,4},{8,11},{9,10},{10,... | collective-permute-start | bytes 294920 | tf_op jit(solution)/shard_map/ppermute | solution.py:20
  41.4 6.1 %collective-permute-start.7 = (f32[192,128]{1,0:T(8,128)S(1)}, f32[192,128]{1,0:T(8,128)S(1)}, u32[]{:S(2)}, u32[]{:S(2)}) collective-permute-start(f32[192,128]{1,0:T(8,128)S(1)} %add_add_fusion.2), channel_id=1, source_target_pairs={{0,2},{1,3},{2,0},{3,1},{4,6},{5,7},{6,4},{7,5},{8,10},{9,11},{10,... | collective-permute-start | bytes 294920 | tf_op jit(solution)/shard_map/ppermute | solution.py:20
  42.0 5.5 %collective-permute-start.6 = (f32[192,128]{1,0:T(8,128)S(1)}, f32[192,128]{1,0:T(8,128)S(1)}, u32[]{:S(2)}, u32[]{:S(2)}) collective-permute-start(f32[192,128]{1,0:T(8,128)S(1)} %add_add_fusion.2), channel_id=1, source_target_pairs={{0,1},{1,0},{2,3},{3,2},{4,5},{5,4},{6,7},{7,6},{8,9},{9,8},{10,11... | collective-permute-start | bytes 294920 | tf_op jit(solution)/shard_map/ppermute | solution.py:20
  47.5 9.6 %collective-permute-start.11 = (f32[192,128]{1,0:T(8,128)S(1)}, f32[192,128]{1,0:T(8,128)S(1)}, u32[]{:S(2)}, u32[]{:S(2)}) collective-permute-start(f32[192,128]{1,0:T(8,128)S(1)} %add_add_fusion.1), channel_id=1, source_target_pairs={{0,24},{4,28},{8,16},{12,20},{16,8},{20,12},{24,0},{28,4},{32,56},... | collective-permute-start | bytes 294920 | tf_op jit(solution)/shard_map/ppermute | solution.py:20
  48.2 8.9 %collective-permute-start.10 = (f32[192,128]{1,0:T(8,128)S(1)}, f32[192,128]{1,0:T(8,128)S(1)}, u32[]{:S(2)}, u32[]{:S(2)}) collective-permute-start(f32[192,128]{1,0:T(8,128)S(1)} %add_add_fusion.1), channel_id=1, source_target_pairs={{0,16},{4,20},{8,24},{12,28},{16,0},{20,4},{24,8},{28,12},{32,48},... | collective-permute-start | bytes 294920 | tf_op jit(solution)/shard_map/ppermute | solution.py:20
  50.9 6.3 %collective-permute-start.9 = (f32[192,128]{1,0:T(8,128)S(1)}, f32[192,128]{1,0:T(8,128)S(1)}, u32[]{:S(2)}, u32[]{:S(2)}) collective-permute-start(f32[192,128]{1,0:T(8,128)S(1)} %add_add_fusion.1), channel_id=1, source_target_pairs={{0,8},{4,12},{8,0},{12,4},{16,24},{20,28},{24,16},{28,20},{32,40},... | collective-permute-start | bytes 294920 | tf_op jit(solution)/shard_map/ppermute | solution.py:20
  52.4 14.5 %all-to-all-start.1 = ((f32[8,24,256]{2,1,0:T(8,128)}), f32[8,24,256]{2,1,0:T(8,128)S(1)}, u32[]{:S(2)}, u32[]{:S(2)}) async-start(f32[8,24,256]{2,1,0:T(8,128)} %reduce_sum.18), calls=%async_computation.1 | async-start | bytes 393216 | tf_op jit(solution)/shard_map/all_to_all | solution.py:223
  57.2 1.4 %collective-permute-start.12 = (f32[192,128]{1,0:T(8,128)S(1)}, f32[192,128]{1,0:T(8,128)S(1)}, u32[]{:S(2)}, u32[]{:S(2)}) collective-permute-start(f32[192,128]{1,0:T(8,128)S(1)} %add_add_fusion.mine), channel_id=1, source_target_pairs={{0,4},{4,0},{8,12},{12,8},{16,20},{20,16},{24,28},{28,24},{32,36},... | collective-permute-start | bytes 294920 | tf_op jit(solution)/shard_map/ppermute | solution.py:20
  66.9 16.2 %collective-permute-start.15 = (f32[24,256]{1,0:T(8,128)S(1)}, f32[24,256]{1,0:T(8,128)S(1)}, u32[]{:S(2)}, u32[]{:S(2)}) collective-permute-start(f32[24,256]{1,0:T(8,128)S(1)} %reduce_sum.19), channel_id=1, source_target_pairs={{0,3},{1,2},{2,1},{3,0},{4,7},{5,6},{6,5},{7,4},{8,11},{9,10},{10,... | collective-permute-start | bytes 73736 | tf_op jit(solution)/shard_map/ppermute | solution.py:20
  68.8 14.3 %collective-permute-start.14 = (f32[24,256]{1,0:T(8,128)S(1)}, f32[24,256]{1,0:T(8,128)S(1)}, u32[]{:S(2)}, u32[]{:S(2)}) collective-permute-start(f32[24,256]{1,0:T(8,128)S(1)} %reduce_sum.19), channel_id=1, source_target_pairs={{0,2},{1,3},{2,0},{3,1},{4,6},{5,7},{6,4},{7,5},{8,10},{9,11},{10,... | collective-permute-start | bytes 73736 | tf_op jit(solution)/shard_map/ppermute | solution.py:20
  69.4 13.7 %collective-permute-start.13 = (f32[24,256]{1,0:T(8,128)S(1)}, f32[24,256]{1,0:T(8,128)S(1)}, u32[]{:S(2)}, u32[]{:S(2)}) collective-permute-start(f32[24,256]{1,0:T(8,128)S(1)} %reduce_sum.19), channel_id=1, source_target_pairs={{0,1},{1,0},{2,3},{3,2},{4,5},{5,4},{6,7},{7,6},{8,9},{9,8},{10,11... | collective-permute-start | bytes 73736 | tf_op jit(solution)/shard_map/ppermute | solution.py:20

commit v2 on v1

v2 whole, which is shorter than its diff:
```python
import functools

import jax
import jax.numpy as jnp
from jax import lax
from jax.experimental import pallas as pl
from jax.experimental.pallas import tpu as pltpu
from jax.sharding import PartitionSpec as P

LANES = 128
SUB = 8
PANEL = 64
CHUNK = 256
LOAD = 512
AHEAD = 2


def barrier(*values):
    return lax.optimization_barrier(values)


def shifted(x, axis, target):
    return lax.ppermute(x, axis, [(i, target(i)) for i in range(lax.axis_size(axis))])


def along_z(target):
    return lambda i: (target(i >> 3) % 8) << 3 | i & 7


Z_PAIR = along_z(lambda z: z ^ 1)
Z_NEXT = along_z(lambda z: z + 1 if z % 2 else z - 1)
Z_TWO = along_z(lambda z: z + 2 if z % 2 else z - 2)
Z_THREE = along_z(lambda z: z + 3 if z % 2 else z - 3)


def along_x(bits):
    return lambda i: i ^ bits << 1


def other_core(i):
    return i ^ 1


def flip(bits):
    return lambda i: i ^ bits


def sum4(parts):
    return (parts[0] + parts[1]) + (parts[2] + parts[3])


def over_four(x, axis, flipped):
    one, three, two = (shifted(x, axis, flipped(k)) for k in (1, 3, 2))
    return sum4([x, one, two, three])


def splat(x, sub=None, lane=None):
    if lane is not None:
        x = x[:, lane : lane + 1]
    if sub is not None:
        x = x[sub : sub + 1, :]
    return jnp.broadcast_to(x, (SUB, LANES))


def sum8(parts):
    return sum4(parts[:4]) + sum4(parts[4:])


def factor_in_place(s, order):
    halves = order // LANES
    row = lax.broadcasted_iota(jnp.int32, (SUB, LANES), 0)
    lane = lax.broadcasted_iota(jnp.int32, (SUB, LANES), 1)

    def tile(r, h):
        return (slice(r, r + SUB), slice(LANES * h, LANES * (h + 1)))

    for p0 in range(0, order, PANEL):
        p1, here = p0 + PANEL, p0 // LANES
        cols = [splat(s[tile(p0, here)], lane=p0 % LANES + k) for k in range(SUB)]
        for r0 in range(p0, p1, SUB):
            l0 = r0 % LANES
            last = r0 + SUB >= p1
            fwd = [s[tile(r0, h)] for h in range(halves)]
            if not last:
                ahead = [splat(fwd[here], lane=l0 + SUB + k) for k in range(SUB)]
                below = s[tile(r0 + SUB, here)]
                next_coef = [splat(below, lane=l0 + k) for k in range(SUB)]
                next_cols = [splat(below, lane=l0 + SUB + k) for k in range(SUB)]
            pivots = (lane >= l0) & (lane < l0 + SUB)
            fwd[here] = jnp.where(pivots, jnp.where(lane - l0 == row, 1.0, 0.0), fwd[here])
            both = list(fwd)
            inv_d = jnp.zeros((SUB, LANES), jnp.float32)
            for i in range(0, SUB, 2):
                j = i + 1
                a, b, c = splat(cols[i], sub=i), splat(cols[i], sub=j), splat(cols[j], sub=j)
                inv_det, inv_a = 1.0 / (a * c - b * b), 1.0 / a
                pair = (row == i) | (row == j)
                ci = jnp.where(row == i, -1.0, jnp.where(row == j, 0.0, cols[i]))
                cj = jnp.where(row == j, -1.0, jnp.where(row == i, 0.0, cols[j]))
                mi = (ci * c - cj * b) * inv_det
                mj = (cj * a - ci * b) * inv_det
                fi = jnp.where(row > j, mi, jnp.where(row == j, b * inv_a, 0.0))
                fj = jnp.where(row > j, mj, 0.0)
                inv_d = jnp.where(row == i, inv_a, jnp.where(row == j, a * inv_det, inv_d))

                def eliminated(x):
                    x_i, x_j = splat(x, sub=i), splat(x, sub=j)
                    return jnp.where(pair, 0.0, x) - (mi * x_i + mj * x_j)

                for k in range(j + 1, SUB):
                    cols[k] = eliminated(cols[k])
                fwd = [x - (fi * splat(x, sub=i) + fj * splat(x, sub=j)) for x in fwd]
                if not last:
                    ahead = [eliminated(x) for x in ahead]
                    both = [eliminated(x) for x in both]
            if not last:
                cols = [
                    next_cols[k] - sum8([next_coef[m] * splat(ahead[k], sub=m) for m in range(SUB)])
                    for k in range(SUB)
                ]
                rows = [[splat(x, sub=k) for x in both] for k in range(SUB)]
                for g0 in range(r0 + SUB, p1, SUB):
                    old = [s[tile(g0, h)] for h in range(halves)]
                    coef = next_coef
                    if g0 > r0 + SUB:
                        coef = [splat(old[here], lane=l0 + k) for k in range(SUB)]
                    old[here] = jnp.where(pivots, 0.0, old[here])
                    for h in range(halves):
                        change = sum8([coef[k] * rows[k][h] for k in range(SUB)])
                        s[tile(g0, h)] = old[h] - change
            scale = jnp.sqrt(inv_d)
            for h in range(halves):
                s[tile(r0, h)] = fwd[h] * scale
        if p1 < order:
            panel = s[p0:p1, :]
            r = lax.broadcasted_iota(jnp.int32, panel.shape, 0)
            c = lax.broadcasted_iota(jnp.int32, panel.shape, 1)
            panel = jnp.where((c < p1) & (c > p0 + r), 0.0, panel)
            update = lax.dot_general(
                panel[:, p1:],
                panel,
                (((0,), (0,)), ((), ())),
                precision=lax.Precision.HIGHEST,
                preferred_element_type=jnp.float32,
            )
            c = lax.broadcasted_iota(jnp.int32, update.shape, 1)
            s[p1:, :] = jnp.where((c >= p0) & (c < p1), 0.0, s[p1:, :]) - update


def factor_kernel(core, mine, other, inv_t, s):
    first = core[0] == 0
    half = mine.shape[0]
    a, b = mine[...], other[...]
    low = jnp.where(first, a, b)
    high = jnp.where(first, b, a)
    s[:LANES, :LANES] = low[:LANES]
    s[: half - LANES, LANES:] = low[LANES:]
    s[half - LANES : LANES, LANES:] = high[: 2 * LANES - half]
    s[LANES:, LANES:] = high[2 * LANES - half :]
    factor_in_place(s, s.shape[0])
    r = lax.broadcasted_iota(jnp.int32, s.shape, 0)
    c = lax.broadcasted_iota(jnp.int32, s.shape, 1)
    inv_t[...] = jnp.where(c <= r, s[...], 0.0)


def factor(core, mine, other):
    order = 2 * LANES
    vmem = pl.BlockSpec(memory_space=pltpu.VMEM)
    return pl.pallas_call(
        factor_kernel,
        out_shape=jax.ShapeDtypeStruct((order, order), jnp.float32),
        in_specs=[pl.BlockSpec(memory_space=pltpu.SMEM), vmem, vmem],
        out_specs=vmem,
        scratch_shapes=[pltpu.VMEM((order, order), jnp.float32)],
        compiler_params=pltpu.CompilerParams(vmem_limit_bytes=16 * 2**20),
        cost_estimate=pl.CostEstimate(flops=0, bytes_accessed=20 * 2**20, transcendentals=0),
    )(core, mine, other)


def basis_kernel(sketch, inv_t, basis, out, sems):
    inv = inv_t[...]
    hi = inv.astype(jnp.bfloat16)
    mid = (inv - hi.astype(jnp.float32)).astype(jnp.bfloat16)
    copies = []
    for n in range(sketch.shape[0] // CHUNK):
        rows = slice(n * CHUNK, (n + 1) * CHUNK)
        x = sketch[rows, :]
        total = None
        for part in (mid, hi):
            term = lax.dot_general(
                x, part, (((1,), (1,)), ((), ())), preferred_element_type=jnp.float32
            )
            total = term if total is None else total + term
        out[rows, :] = total
        copies.append(pltpu.make_async_copy(out.at[rows, :], basis.at[rows, :], sems.at[n]))
        copies[-1].start()
    for copy in copies:
        copy.wait()


def basis_of(sketch, inv_t):
    rows, order = sketch.shape
    vmem = pl.BlockSpec(memory_space=pltpu.VMEM)
    return pl.pallas_call(
        basis_kernel,
        out_shape=jax.ShapeDtypeStruct((rows, order), jnp.float32),
        in_specs=[vmem, vmem],
        out_specs=pl.BlockSpec(memory_space=pl.ANY),
        scratch_shapes=[
            pltpu.VMEM((rows, order), jnp.float32),
            pltpu.SemaphoreType.DMA((rows // CHUNK,)),
        ],
        compiler_params=pltpu.CompilerParams(vmem_limit_bytes=16 * 2**20),
        cost_estimate=pl.CostEstimate(
            flops=4 * rows * order * order, bytes_accessed=6 * rows * order, transcendentals=0
        ),
    )(sketch, inv_t)


def front_kernel(core, e, t, sketch, mine, theirs, kept, given, e_kept, t_kept, sems, *, scale):
    steps = e.shape[0] // LOAD
    load_t = pltpu.make_async_copy(t, t_kept, sems.at[steps])
    load_t.start()
    blocks = [slice(n * LOAD, (n + 1) * LOAD) for n in range(steps)]
    loads = [
        pltpu.make_async_copy(e.at[rows, :], e_kept.at[rows, :], sems.at[n])
        for n, rows in enumerate(blocks)
    ]
    for load in loads[:AHEAD]:
        load.start()
    load_t.wait()
    for n, rows in enumerate(blocks):
        loads[n].wait()
        if n + AHEAD < steps:
            loads[n + AHEAD].start()
        sketch[rows, :] = jnp.dot(
            e_kept[rows, :], t_kept[...], preferred_element_type=jnp.float32
        ).astype(jnp.bfloat16)
    s = sketch[...]
    by_rows = (((0,), (0,)), ((), ()))
    gram = lax.dot_general(s, s, by_rows, preferred_element_type=jnp.float32)
    packed = [gram[:LANES, :LANES], gram[:LANES, LANES:], gram[LANES:, LANES:]]
    packed = jnp.concatenate(packed, axis=0) * scale
    half = packed.shape[0] // 2
    first = core[0] == 0
    mine[...] = jnp.where(first, packed[:half], packed[half:])
    theirs[...] = jnp.where(first, packed[half:], packed[:half])
    n_x, n_z, owned, order = kept.shape
    per_z = 2 * n_x * owned
    for z in range(0, n_z, 2):
        feats = slice(z * per_z, (z + 2) * per_z)
        c = lax.dot_general(
            e_kept[:, feats], s, by_rows, preferred_element_type=jnp.float32
        )
        c = c.reshape(2, n_x, 2, owned, order)
        for dz in range(2):
            for x in range(n_x):
                kept[x, z + dz] = jnp.where(first, c[dz, x, 0], c[dz, x, 1])
                given[x, z + dz] = jnp.where(first, c[dz, x, 1], c[dz, x, 0])


def front(core, e, t, rows_total, n_x, n_z):
    rows, feats = e.shape
    order = t.shape[1]
    gram_half = jax.ShapeDtypeStruct((3 * LANES // 2, LANES), jnp.float32)
    owned = feats // (2 * n_x * n_z)
    cross_half = jax.ShapeDtypeStruct((n_x, n_z, owned, order), jnp.float32)
    vmem = pl.BlockSpec(memory_space=pltpu.VMEM)
    hbm = pl.BlockSpec(memory_space=pltpu.HBM)
    return pl.pallas_call(
        functools.partial(front_kernel, scale=1.0 / rows_total),
        out_shape=(
            jax.ShapeDtypeStruct((rows, order), jnp.bfloat16),
            gram_half,
            gram_half,
            cross_half,
            cross_half,
        ),
        in_specs=[pl.BlockSpec(memory_space=pltpu.SMEM), hbm, hbm],
        out_specs=(vmem,) * 5,
        scratch_shapes=[
            pltpu.VMEM(e.shape, e.dtype),
            pltpu.VMEM(t.shape, t.dtype),
            pltpu.SemaphoreType.DMA((rows // LOAD + 1,)),
        ],
        compiler_params=pltpu.CompilerParams(vmem_limit_bytes=52 * 2**20),
    )(core, e, t)


def pick(x, index):
    return lax.dynamic_index_in_dim(x, index, 0, keepdims=False)


def body(embeddings, test_matrix):
    n_wide = lax.axis_size("wide")
    rows_total = embeddings.shape[0] * n_wide * lax.axis_size("narrow")
    place = lax.axis_index("wide")
    core, x_at, z_at = place & 1, place >> 1 & 3, place >> 3
    at = core.reshape(1)
    sketch, mine, theirs, kept, given = front(at, embeddings, test_matrix, rows_total, 4, 8)
    groups_x = [[z * 8 + x * 2 + c for x in range(4)] for z in range(8) for c in range(2)]
    groups_z = [[z * 8 + r for z in range(8)] for r in range(8)]
    mine = mine + shifted(theirs, "wide", other_core)
    kept = kept + shifted(given, "wide", other_core)
    kept = lax.all_to_all(kept, "wide", 0, 0, tiled=True, axis_index_groups=groups_x)
    mine = mine + shifted(mine, "wide", Z_PAIR)
    mine, = barrier(mine)
    mine = sum4([mine] + [shifted(mine, "wide", t) for t in (Z_NEXT, Z_TWO, Z_THREE)])
    kept = jnp.sum(kept, axis=0)
    kept = lax.all_to_all(kept, "wide", 0, 0, tiled=True, axis_index_groups=groups_z)
    mine, = barrier(mine)
    mine = over_four(mine, "narrow", flip)
    mine, = barrier(mine)
    mine = over_four(mine, "wide", along_x)
    mine, = barrier(mine)
    other = shifted(mine, "wide", other_core)
    inv_t = factor(at, mine, other)
    inv_t, kept = barrier(inv_t, kept)
    kept = jnp.sum(kept, axis=0)
    kept = over_four(kept, "narrow", flip)
    basis_rows = basis_of(sketch, inv_t)
    loadings = (
        lax.dot_general(
            kept, inv_t, (((1,), (1,)), ((), ())), precision=lax.Precision.HIGHEST
        )
        / rows_total
    )
    return (basis_rows, loadings)


CROSS = "a2a"


def solution(mesh):
    in_specs = (P(("wide", "narrow"), None), P())
    out_specs = (P(("wide", "narrow"), None), P("wide", None))
    return jax.shard_map(body, mesh=mesh, in_specs=in_specs, out_specs=out_specs, check_vma=False)
```

time: 84.5 us -> 68.5 us (0.81)
  matrix products: 11.7 us -> 0.94 us
  local copies, waits for them, and re-layouts: 3.98 us -> 0.01 us
  waiting for transfers between devices: 17.7 us -> 13.9 us
  Pallas kernels: 11.8 us -> 15.5 us
  other arithmetic: 2.82 us -> 1.84 us
    dot_general x3 -> x0, matrix products: 10.8 us -> none  [the longest x1 5.73 us: body(): lax.dot_general(embeddings, sketch, (((0,), (0,)), ((), ())), preferred_e...]
    all_to_all x1, waiting for transfers between devices: 8.33 us -> 1.47 us  [body(): lax.all_to_all(kept, 'wide', 0, 0, tiled=True, axis_index_groups=groups_z)]
    pallas_call x1 -> x3, Pallas kernels: 11.8 us -> 15.5 us  [the longest x1 7.13 us: front(): pl.pallas_call(functools.partial(front_kernel, scale=1.0 / rows_total), o...]
    ppermute x16, waiting for transfers between devices: 9.41 us -> 12.5 us  [shifted(): lax.ppermute(x, axis, [(i, target(i)) for i in range(lax.axis_size(axis))])]
    dot_general x1 -> x0, local copies, waits for them, and re-layouts: 1.87 us -> none  [body(): lax.dot_general(embeddings, sketch, (((0,), (0,)), ((), ())), preferred_e...]
    unnamed x6 -> x2, local copies, waits for them, and re-layouts: 1.14 us -> 0.01 us
    add x0 -> x1, other arithmetic: none -> 1 us  [body(): kept = kept + shifted(given, 'wide', other_core)]
    optimization_barrier x1 -> x0, local copies, waits for them, and re-layouts: 0.95 us -> none  [barrier(): return lax.optimization_barrier(values)]
  transfers between devices with their start and end apart: 18 -> 18, of which waited for: 5 -> 7; matrix products, arithmetic and copies ran while one was open for 11% -> 3% of each run, Pallas kernels for 14% -> 12%
where the time goes in v2:
time: 68.5 us; the launch traced here: 68.2 us
  starting transfers between devices  35.2 us (51%)
  Pallas kernels  15.5 us (23%)
  waiting for transfers between devices  13.9 us (20%)
  other arithmetic  1.84 us (3%)
  matrix products  0.94 us (1%)
  between operations  0.75 us (1%)
    ppermute x16, starting transfers between devices, shifted(): lax.ppermute(x, axis, [(i, target(i)) for i in range(lax.axis_size(axis))])  25.7 us
    ppermute x16, waiting for transfers between devices, shifted(): lax.ppermute(x, axis, [(i, target(i)) for i in range(lax.axis_size(axis))])  12.5 us
    pallas_call x1, Pallas kernels, front(): pl.pallas_call(functools.partial(front_kernel, scale=1.0 / rows_total), o...  7.13 us
    pallas_call x1, Pallas kernels, factor(): pl.pallas_call(factor_kernel, out_shape=jax.ShapeDtypeStruct((order, orde...  6.68 us
    all_to_all x1, starting transfers between devices, body(): lax.all_to_all(kept, 'wide', 0, 0, tiled=True, axis_index_groups=groups_x)  4.8 us
    all_to_all x1, starting transfers between devices, body(): lax.all_to_all(kept, 'wide', 0, 0, tiled=True, axis_index_groups=groups_z)  4.67 us
    pallas_call x1, Pallas kernels, basis_of(): pl.pallas_call(basis_kernel, out_shape=jax.ShapeDtypeStruct((rows, order)...  1.71 us
    all_to_all x1, waiting for transfers between devices, body(): lax.all_to_all(kept, 'wide', 0, 0, tiled=True, axis_index_groups=groups_z)  1.47 us
  transfers between devices with their start and end apart: 18, of which 7 were waited for; matrix products, arithmetic and copies ran while one was open for 3% of the time, Pallas kernels for 12%

profile of v2, /device:TPU:4, one launch (start us, length us, event | category | flops | bytes accessed | tf_op | source)
XLA Modules:
  0.0 68.2 jit_solution(4204748993490133620)
XLA Ops:
  0.6 7.1 %shard_map.41 = (bf16[2048,256]{1,0:T(8,128)(2,1)}, f32[192,128]{1,0:T(8,128)S(1)}, f32[192,128]{1,0:T(8,128)S(1)}, f32[4,8,24,256]{3,2,1,0:T(8,128)S(1)}, f32[4,8,24,256]{3,2,1,0:T(8,128)S(1)}) custom-call(s32[1]{0:T(128)} %bitcast.core, bf16[2048,1536]{1,0:T(8,128)(2,1)} %e.1, bf16[1536,256]{1,0:T(8,128)(2,1)} %t.1), custom_call_target="tpu_custom_call" | custom-call | tf_op jit(solution)/shard_map/pallas_call | solution.py:270
  8.4 1.9 %collective-permute-done = f32[192,128]{1,0:T(8,128)S(1)} collective-permute-done((f32[192,128]{1,0:T(8,128)S(1)}, f32[192,128]{1,0:T(8,128)S(1)}, u32[]{:S(2)}, u32[]{:S(2)}) %collective-permute-start) | collective-permute-done | bytes 98336 | tf_op jit(solution)/shard_map/ppermute | solution.py:23
  10.3 2.0 %collective-permute-start.1 = (f32[192,128]{1,0:T(8,128)S(1)}, f32[192,128]{1,0:T(8,128)S(1)}, u32[]{:S(2)}, u32[]{:S(2)}) collective-permute-start(f32[192,128]{1,0:T(8,128)S(1)} %add.45), channel_id=1, source_target_pairs={{0,32},{4,36},{8,40},{12,44},{16,48},{20,52},{24,56},{28,60},{32,0... | collective-permute-start | bytes 294920 | tf_op jit(solution)/shard_map/ppermute | solution.py:23
  12.3 3.1 %collective-permute-done.1 = f32[192,128]{1,0:T(8,128)S(1)} collective-permute-done((f32[192,128]{1,0:T(8,128)S(1)}, f32[192,128]{1,0:T(8,128)S(1)}, u32[]{:S(2)}, u32[]{:S(2)}) %collective-permute-start.1) | collective-permute-done | bytes 98336 | tf_op jit(solution)/shard_map/ppermute | solution.py:23
  15.4 6.7 %collective-permute-start.4 = (f32[192,128]{1,0:T(8,128)S(1)}, f32[192,128]{1,0:T(8,128)S(1)}, u32[]{:S(2)}, u32[]{:S(2)}) collective-permute-start(f32[192,128]{1,0:T(8,128)S(1)} %add.46), channel_id=1, source_target_pairs={{0,160},{4,164},{8,168},{12,172},{16,176},{20,180},{24,184},{28,18... | collective-permute-start | bytes 294920 | tf_op jit(solution)/shard_map/ppermute | solution.py:23
  22.6 3.1 %collective-permute-start.2 = (f32[192,128]{1,0:T(8,128)S(1)}, f32[192,128]{1,0:T(8,128)S(1)}, u32[]{:S(2)}, u32[]{:S(2)}) collective-permute-start(f32[192,128]{1,0:T(8,128)S(1)} %add.46), channel_id=1, source_target_pairs={{0,224},{4,228},{8,232},{12,236},{16,240},{20,244},{24,248},{28,25... | collective-permute-start | bytes 294920 | tf_op jit(solution)/shard_map/ppermute | solution.py:23
  25.8 1.0 %add.56 = f32[4,8,24,256]{3,2,1,0:T(8,128)} add(f32[4,8,24,256]{3,2,1,0:T(8,128)S(1)} %get-tuple-element.12, f32[4,8,24,256]{3,2,1,0:T(8,128)S(1)} %collective-permute-done.12) | non-fusion elementwise | flops 196608 | bytes 2359296 | tf_op jit(solution)/shard_map/add | solution.py:304
  26.8 4.8 %all-to-all-start = ((f32[4,8,24,256]{3,2,1,0:T(8,128)}), f32[4,8,24,256]{3,2,1,0:T(8,128)S(1)}, u32[]{:S(2)}, u32[]{:S(2)}) async-start(f32[4,8,24,256]{3,2,1,0:T(8,128)} %add.56), calls=%async_computation | async-start | bytes 1572864 | tf_op jit(solution)/shard_map/all_to_all | solution.py:305
  31.6 3.1 %collective-permute-start.7 = (f32[192,128]{1,0:T(8,128)S(1)}, f32[192,128]{1,0:T(8,128)S(1)}, u32[]{:S(2)}, u32[]{:S(2)}) collective-permute-start(f32[192,128]{1,0:T(8,128)S(1)} %add_add_fusion.2), channel_id=1, source_target_pairs={{0,3},{1,2},{2,1},{3,0},{4,7},{5,6},{6,5},{7,4},{8,11},{9,10},{10,... | collective-permute-start | bytes 294920 | tf_op jit(solution)/shard_map/ppermute | solution.py:23
  35.8 2.7 %collective-permute-done.7 = f32[192,128]{1,0:T(8,128)S(1)} collective-permute-done((f32[192,128]{1,0:T(8,128)S(1)}, f32[192,128]{1,0:T(8,128)S(1)}, u32[]{:S(2)}, u32[]{:S(2)}) %collective-permute-start.7) | collective-permute-done | bytes 98336 | tf_op jit(solution)/shard_map/ppermute | solution.py:23
  38.6 2.3 %collective-permute-done.6 = f32[192,128]{1,0:T(8,128)S(1)} collective-permute-done((f32[192,128]{1,0:T(8,128)S(1)}, f32[192,128]{1,0:T(8,128)S(1)}, u32[]{:S(2)}, u32[]{:S(2)}) %collective-permute-start.6) | collective-permute-done | bytes 98336 | tf_op jit(solution)/shard_map/ppermute | solution.py:23
  40.9 0.6 collective-permute-start.10
  41.5 2.7 %collective-permute-start.9 = (f32[192,128]{1,0:T(8,128)S(1)}, f32[192,128]{1,0:T(8,128)S(1)}, u32[]{:S(2)}, u32[]{:S(2)}) collective-permute-start(f32[192,128]{1,0:T(8,128)S(1)} %add_add_fusion.1), channel_id=1, source_target_pairs={{0,16},{4,20},{8,24},{12,28},{16,0},{20,4},{24,8},{28,12},{32,48},... | collective-permute-start | bytes 294920 | tf_op jit(solution)/shard_map/ppermute | solution.py:23
  44.2 0.9 %collective-permute-start.8 = (f32[192,128]{1,0:T(8,128)S(1)}, f32[192,128]{1,0:T(8,128)S(1)}, u32[]{:S(2)}, u32[]{:S(2)}) collective-permute-start(f32[192,128]{1,0:T(8,128)S(1)} %add_add_fusion.1), channel_id=1, source_target_pairs={{0,8},{4,12},{8,0},{12,4},{16,24},{20,28},{24,16},{28,20},{32,40},... | collective-permute-start | bytes 294920 | tf_op jit(solution)/shard_map/ppermute | solution.py:23
  45.1 0.7 %reduce_sum.18 = f32[8,24,256]{2,1,0:T(8,128)} reduce(f32[4,8,24,256]{3,2,1,0:T(8,128)S(1)} %all-to-all-done, f32[]{:T(128)} %constant.11.clone.1), dimensions={0}, to_apply=%region_0.0 | reduce | flops 147456 | bytes 983044 | tf_op jit(solution)/shard_map/reduce_sum | solution.py:309
  45.8 4.7 %all-to-all-start.1 = ((f32[8,24,256]{2,1,0:T(8,128)}), f32[8,24,256]{2,1,0:T(8,128)S(1)}, u32[]{:S(2)}, u32[]{:S(2)}) async-start(f32[8,24,256]{2,1,0:T(8,128)} %reduce_sum.18), calls=%async_computation.1 | async-start | bytes 393216 | tf_op jit(solution)/shard_map/all_to_all | solution.py:310
  50.8 1.3 %collective-permute-done.11.other = f32[192,128]{1,0:T(8,128)S(1)} collective-permute-done((f32[192,128]{1,0:T(8,128)S(1)}, f32[192,128]{1,0:T(8,128)S(1)}, u32[]{:S(2)}, u32[]{:S(2)}) %collective-permute-start.11) | collective-permute-done | bytes 98336 | tf_op jit(solution)/shard_map/ppermute | solution.py:23
  52.1 6.7 %shard_map.42.inv_t = f32[256,256]{1,0:T(8,128)S(1)} custom-call(s32[1]{0:T(128)} %bitcast.core, f32[192,128]{1,0:T(8,128)S(1)} %add_add_fusion.mine, f32[192,128]{1,0:T(8,128)S(1)} %collective-permute-done.11.other), custom_call_target="tpu_custom_call" | custom-call | bytes 20971520 | tf_op jit(solution)/shard_map/pallas_call | solution.py:169
  58.8 1.5 %all-to-all-done.1 = f32[8,24,256]{2,1,0:T(8,128)S(1)} async-done(((f32[8,24,256]{2,1,0:T(8,128)}), f32[8,24,256]{2,1,0:T(8,128)S(1)}, u32[]{:S(2)}, u32[]{:S(2)}) %all-to-all-start.1) | async-done | bytes 196640 | tf_op jit(solution)/shard_map/all_to_all | solution.py:310
  60.2 1.7 %collective-permute-start.15 = (f32[24,256]{1,0:T(8,128)S(1)}, f32[24,256]{1,0:T(8,128)S(1)}, u32[]{:S(2)}, u32[]{:S(2)}) collective-permute-start(f32[24,256]{1,0:T(8,128)S(1)} %reduce_sum.19), channel_id=1, source_target_pairs={{0,3},{1,2},{2,1},{3,0},{4,7},{5,6},{6,5},{7,4},{8,11},{9,10},{10,... | collective-permute-start | bytes 73736 | tf_op jit(solution)/shard_map/ppermute | solution.py:23
  62.6 1.9 %collective-permute-start.13 = (f32[24,256]{1,0:T(8,128)S(1)}, f32[24,256]{1,0:T(8,128)S(1)}, u32[]{:S(2)}, u32[]{:S(2)}) collective-permute-start(f32[24,256]{1,0:T(8,128)S(1)} %reduce_sum.19), channel_id=1, source_target_pairs={{0,1},{1,0},{2,3},{3,2},{4,5},{5,4},{6,7},{7,6},{8,9},{9,8},{10,11... | collective-permute-start | bytes 73736 | tf_op jit(solution)/shard_map/ppermute | solution.py:23
  64.4 1.7 %shard_map.43 = f32[2048,256]{1,0:T(8,128)} custom-call(bf16[2048,256]{1,0:T(8,128)(2,1)S(1)} %copy-done, f32[256,256]{1,0:T(8,128)S(1)} %shard_map.42.inv_t), custom_call_target="tpu_custom_call" | custom-call | flops 536870912 | bytes 3145728 | tf_op jit(solution)/shard_map/pallas_call | solution.py:204
  66.2 1.1 %collective-permute-done.14 = f32[24,256]{1,0:T(8,128)S(1)} collective-permute-done((f32[24,256]{1,0:T(8,128)S(1)}, f32[24,256]{1,0:T(8,128)S(1)}, u32[]{:S(2)}, u32[]{:S(2)}) %collective-permute-start.14) | collective-permute-done | bytes 24608 | tf_op jit(solution)/shard_map/ppermute | solution.py:23
  67.3 0.9 %convolution_multiply_fusion = f32[24,256]{1,0:T(8,128)} fusion(f32[256,256]{1,0:T(8,128)S(1)} %shard_map.42.inv_t, f32[24,256]{1,0:T(8,128)S(1)} %collective-permute-done.14, f32[24,256]{1,0:T(8,128)S(1)} %collective-permute-done.15, f32[24,256]{1,0:T(8,128)S(1)} %reduce_sum.19, f32[24,256]{1,0:T(8,128)S(1)} %collective-permute-done.13), kind=kOutput, calls=%fused_computation | convolution fusion | flops 18898944 | bytes 385024 | tf_op jit(solution)/shard_map/dot_general | solution.py:323
  (26 shorter events, 3.3 us)
Async XLA Ops:
  7.8 56.7 %copy-start = (bf16[2048,256]{1,0:T(8,128)(2,1)S(1)}, bf16[2048,256]{1,0:T(8,128)(2,1)}, u32[]{:S(2)}) copy-start(bf16[2048,256]{1,0:T(8,128)(2,1)} %get-tuple-element.9.sketch) | copy-start | bytes 3145732
  7.8 18.0 %collective-permute-start.12 = (f32[4,8,24,256]{3,2,1,0:T(8,128)S(1)}, f32[4,8,24,256]{3,2,1,0:T(8,128)S(1)}, u32[]{:S(2)}, u32[]{:S(2)}) collective-permute-start(f32[4,8,24,256]{3,2,1,0:T(8,128)S(1)} %get-tuple-element.13), channel_id=1, source_target_pairs={{0,4},{4,0},{8,12},{12,8},{16,20},{20,16},{24,28},{28,24},{32,36},... | collective-permute-start | bytes 2359304 | tf_op jit(solution)/shard_map/ppermute | solution.py:23
  7.9 2.4 %collective-permute-start = (f32[192,128]{1,0:T(8,128)S(1)}, f32[192,128]{1,0:T(8,128)S(1)}, u32[]{:S(2)}, u32[]{:S(2)}) collective-permute-start(f32[192,128]{1,0:T(8,128)S(1)} %get-tuple-element.11), channel_id=1, source_target_pairs={{0,4},{4,0},{8,12},{12,8},{16,20},{20,16},{24,28},{28,24},{32,36},... | collective-permute-start | bytes 294920 | tf_op jit(solution)/shard_map/ppermute | solution.py:23
  10.3 5.1 %collective-permute-start.1 = (f32[192,128]{1,0:T(8,128)S(1)}, f32[192,128]{1,0:T(8,128)S(1)}, u32[]{:S(2)}, u32[]{:S(2)}) collective-permute-start(f32[192,128]{1,0:T(8,128)S(1)} %add.45), channel_id=1, source_target_pairs={{0,32},{4,36},{8,40},{12,44},{16,48},{20,52},{24,56},{28,60},{32,0... | collective-permute-start | bytes 294920 | tf_op jit(solution)/shard_map/ppermute | solution.py:23
  15.4 16.1 %collective-permute-start.4 = (f32[192,128]{1,0:T(8,128)S(1)}, f32[192,128]{1,0:T(8,128)S(1)}, u32[]{:S(2)}, u32[]{:S(2)}) collective-permute-start(f32[192,128]{1,0:T(8,128)S(1)} %add.46), channel_id=1, source_target_pairs={{0,160},{4,164},{8,168},{12,172},{16,176},{20,180},{24,184},{28,18... | collective-permute-start | bytes 294920 | tf_op jit(solution)/shard_map/ppermute | solution.py:23
  22.1 9.5 %collective-permute-start.3 = (f32[192,128]{1,0:T(8,128)S(1)}, f32[192,128]{1,0:T(8,128)S(1)}, u32[]{:S(2)}, u32[]{:S(2)}) collective-permute-start(f32[192,128]{1,0:T(8,128)S(1)} %add.46), channel_id=1, source_target_pairs={{0,192},{4,196},{8,200},{12,204},{16,208},{20,212},{24,216},{28,22... | collective-permute-start | bytes 294920 | tf_op jit(solution)/shard_map/ppermute | solution.py:23
  22.6 8.9 %collective-permute-start.2 = (f32[192,128]{1,0:T(8,128)S(1)}, f32[192,128]{1,0:T(8,128)S(1)}, u32[]{:S(2)}, u32[]{:S(2)}) collective-permute-start(f32[192,128]{1,0:T(8,128)S(1)} %add.46), channel_id=1, source_target_pairs={{0,224},{4,228},{8,232},{12,236},{16,240},{20,244},{24,248},{28,25... | collective-permute-start | bytes 294920 | tf_op jit(solution)/shard_map/ppermute | solution.py:23
  26.8 18.3 %all-to-all-start = ((f32[4,8,24,256]{3,2,1,0:T(8,128)}), f32[4,8,24,256]{3,2,1,0:T(8,128)S(1)}, u32[]{:S(2)}, u32[]{:S(2)}) async-start(f32[4,8,24,256]{3,2,1,0:T(8,128)} %add.56), calls=%async_computation | async-start | bytes 1572864 | tf_op jit(solution)/shard_map/all_to_all | solution.py:305
  31.6 6.9 %collective-permute-start.7 = (f32[192,128]{1,0:T(8,128)S(1)}, f32[192,128]{1,0:T(8,128)S(1)}, u32[]{:S(2)}, u32[]{:S(2)}) collective-permute-start(f32[192,128]{1,0:T(8,128)S(1)} %add_add_fusion.2), channel_id=1, source_target_pairs={{0,3},{1,2},{2,1},{3,0},{4,7},{5,6},{6,5},{7,4},{8,11},{9,10},{10,... | collective-permute-start | bytes 294920 | tf_op jit(solution)/shard_map/ppermute | solution.py:23
  34.7 6.1 %collective-permute-start.6 = (f32[192,128]{1,0:T(8,128)S(1)}, f32[192,128]{1,0:T(8,128)S(1)}, u32[]{:S(2)}, u32[]{:S(2)}) collective-permute-start(f32[192,128]{1,0:T(8,128)S(1)} %add_add_fusion.2), channel_id=1, source_target_pairs={{0,2},{1,3},{2,0},{3,1},{4,6},{5,7},{6,4},{7,5},{8,10},{9,11},{10,... | collective-permute-start | bytes 294920 | tf_op jit(solution)/shard_map/ppermute | solution.py:23
  35.4 5.5 %collective-permute-start.5 = (f32[192,128]{1,0:T(8,128)S(1)}, f32[192,128]{1,0:T(8,128)S(1)}, u32[]{:S(2)}, u32[]{:S(2)}) collective-permute-start(f32[192,128]{1,0:T(8,128)S(1)} %add_add_fusion.2), channel_id=1, source_target_pairs={{0,1},{1,0},{2,3},{3,2},{4,5},{5,4},{6,7},{7,6},{8,9},{9,8},{10,11... | collective-permute-start | bytes 294920 | tf_op jit(solution)/shard_map/ppermute | solution.py:23
  40.9 9.6 %collective-permute-start.10 = (f32[192,128]{1,0:T(8,128)S(1)}, f32[192,128]{1,0:T(8,128)S(1)}, u32[]{:S(2)}, u32[]{:S(2)}) collective-permute-start(f32[192,128]{1,0:T(8,128)S(1)} %add_add_fusion.1), channel_id=1, source_target_pairs={{0,24},{4,28},{8,16},{12,20},{16,8},{20,12},{24,0},{28,4},{32,56},... | collective-permute-start | bytes 294920 | tf_op jit(solution)/shard_map/ppermute | solution.py:23
  41.5 8.9 %collective-permute-start.9 = (f32[192,128]{1,0:T(8,128)S(1)}, f32[192,128]{1,0:T(8,128)S(1)}, u32[]{:S(2)}, u32[]{:S(2)}) collective-permute-start(f32[192,128]{1,0:T(8,128)S(1)} %add_add_fusion.1), channel_id=1, source_target_pairs={{0,16},{4,20},{8,24},{12,28},{16,0},{20,4},{24,8},{28,12},{32,48},... | collective-permute-start | bytes 294920 | tf_op jit(solution)/shard_map/ppermute | solution.py:23
  44.2 6.3 %collective-permute-start.8 = (f32[192,128]{1,0:T(8,128)S(1)}, f32[192,128]{1,0:T(8,128)S(1)}, u32[]{:S(2)}, u32[]{:S(2)}) collective-permute-start(f32[192,128]{1,0:T(8,128)S(1)} %add_add_fusion.1), channel_id=1, source_target_pairs={{0,8},{4,12},{8,0},{12,4},{16,24},{20,28},{24,16},{28,20},{32,40},... | collective-permute-start | bytes 294920 | tf_op jit(solution)/shard_map/ppermute | solution.py:23
  45.8 14.4 %all-to-all-start.1 = ((f32[8,24,256]{2,1,0:T(8,128)}), f32[8,24,256]{2,1,0:T(8,128)S(1)}, u32[]{:S(2)}, u32[]{:S(2)}) async-start(f32[8,24,256]{2,1,0:T(8,128)} %reduce_sum.18), calls=%async_computation.1 | async-start | bytes 393216 | tf_op jit(solution)/shard_map/all_to_all | solution.py:310
  50.5 1.6 %collective-permute-start.11 = (f32[192,128]{1,0:T(8,128)S(1)}, f32[192,128]{1,0:T(8,128)S(1)}, u32[]{:S(2)}, u32[]{:S(2)}) collective-permute-start(f32[192,128]{1,0:T(8,128)S(1)} %add_add_fusion.mine), channel_id=1, source_target_pairs={{0,4},{4,0},{8,12},{12,8},{16,20},{20,16},{24,28},{28,24},{32,36},... | collective-permute-start | bytes 294920 | tf_op jit(solution)/shard_map/ppermute | solution.py:23
  60.2 5.9 %collective-permute-start.15 = (f32[24,256]{1,0:T(8,128)S(1)}, f32[24,256]{1,0:T(8,128)S(1)}, u32[]{:S(2)}, u32[]{:S(2)}) collective-permute-start(f32[24,256]{1,0:T(8,128)S(1)} %reduce_sum.19), channel_id=1, source_target_pairs={{0,3},{1,2},{2,1},{3,0},{4,7},{5,6},{6,5},{7,4},{8,11},{9,10},{10,... | collective-permute-start | bytes 73736 | tf_op jit(solution)/shard_map/ppermute | solution.py:23
  61.9 5.3 %collective-permute-start.14 = (f32[24,256]{1,0:T(8,128)S(1)}, f32[24,256]{1,0:T(8,128)S(1)}, u32[]{:S(2)}, u32[]{:S(2)}) collective-permute-start(f32[24,256]{1,0:T(8,128)S(1)} %reduce_sum.19), channel_id=1, source_target_pairs={{0,2},{1,3},{2,0},{3,1},{4,6},{5,7},{6,4},{7,5},{8,10},{9,11},{10,... | collective-permute-start | bytes 73736 | tf_op jit(solution)/shard_map/ppermute | solution.py:23
  62.6 4.7 %collective-permute-start.13 = (f32[24,256]{1,0:T(8,128)S(1)}, f32[24,256]{1,0:T(8,128)S(1)}, u32[]{:S(2)}, u32[]{:S(2)}) collective-permute-start(f32[24,256]{1,0:T(8,128)S(1)} %reduce_sum.19), channel_id=1, source_target_pairs={{0,1},{1,0},{2,3},{3,2},{4,5},{5,4},{6,7},{7,6},{8,9},{9,8},{10,11... | collective-permute-start | bytes 73736 | tf_op jit(solution)/shard_map/ppermute | solution.py:23

commit v3 on v2

--- a/solution.py
+++ b/solution.py
@@ -149,14 +149,8 @@
 
 def factor_kernel(core, mine, other, inv_t, s):
     first = core[0] == 0
-    half = mine.shape[0]
     a, b = mine[...], other[...]
-    low = jnp.where(first, a, b)
-    high = jnp.where(first, b, a)
-    s[:LANES, :LANES] = low[:LANES]
-    s[: half - LANES, LANES:] = low[LANES:]
-    s[half - LANES : LANES, LANES:] = high[: 2 * LANES - half]
-    s[LANES:, LANES:] = high[2 * LANES - half :]
+    unpack(s, jnp.concatenate([jnp.where(first, a, b), jnp.where(first, b, a)], axis=0))
     factor_in_place(s, s.shape[0])
     r = lax.broadcasted_iota(jnp.int32, s.shape, 0)
     c = lax.broadcasted_iota(jnp.int32, s.shape, 1)
@@ -215,6 +209,25 @@
             flops=4 * rows * order * order, bytes_accessed=6 * rows * order, transcendentals=0
         ),
     )(sketch, inv_t)
+
+
+def pack(gram):
+    left, right = gram[:, :LANES], gram[:, LANES:]
+    corners = jnp.where(
+        lax.broadcasted_iota(jnp.int32, (PANEL, LANES), 1) < PANEL,
+        pltpu.roll(right[3 * PANEL :], PANEL, 1),
+        left[PANEL : 2 * PANEL],
+    )
+    return jnp.concatenate([left[:PANEL], corners, right[: 3 * PANEL]], axis=0)
+
+
+def unpack(s, packed):
+    corners = packed[PANEL : 2 * PANEL]
+    s[:PANEL, :LANES] = packed[:PANEL]
+    s[PANEL : 2 * PANEL, :LANES] = corners
+    s[: 3 * PANEL, LANES:] = packed[2 * PANEL :]
+    s[3 * PANEL :, LANES:] = pltpu.roll(corners, PANEL, 1)
+    s[2 * PANEL :, :LANES] = jnp.zeros_like(corners, shape=(2 * PANEL, LANES))
 
 
 def front_kernel(core, e, t, sketch, mine, theirs, kept, given, e_kept, t_kept, sems, *, scale):
@@ -239,8 +252,7 @@
     s = sketch[...]
     by_rows = (((0,), (0,)), ((), ()))
     gram = lax.dot_general(s, s, by_rows, preferred_element_type=jnp.float32)
-    packed = [gram[:LANES, :LANES], gram[:LANES, LANES:], gram[LANES:, LANES:]]
-    packed = jnp.concatenate(packed, axis=0) * scale
+    packed = pack(gram * scale)
     half = packed.shape[0] // 2
     first = core[0] == 0
     mine[...] = jnp.where(first, packed[:half], packed[half:])
@@ -262,7 +274,7 @@
 def front(core, e, t, rows_total, n_x, n_z):
     rows, feats = e.shape
     order = t.shape[1]
-    gram_half = jax.ShapeDtypeStruct((3 * LANES // 2, LANES), jnp.float32)
+    gram_half = jax.ShapeDtypeStruct((5 * PANEL // 2, LANES), jnp.float32)
     owned = feats // (2 * n_x * n_z)
     cross_half = jax.ShapeDtypeStruct((n_x, n_z, owned, order), jnp.float32)
     vmem = pl.BlockSpec(memory_space=pltpu.VMEM)
@@ -301,6 +313,7 @@
     groups_x = [[z * 8 + x * 2 + c for x in range(4)] for z in range(8) for c in range(2)]
     groups_z = [[z * 8 + r for z in range(8)] for r in range(8)]
     mine = mine + shifted(theirs, "wide", other_core)
+    mine, given = barrier(mine, given)
     kept = kept + shifted(given, "wide", other_core)
     kept = lax.all_to_all(kept, "wide", 0, 0, tiled=True, axis_index_groups=groups_x)
     mine = mine + shifted(mine, "wide", Z_PAIR)

time: 68.5 us -> 65.8 us (0.961)
  starting transfers between devices: 35.2 us -> 33.7 us
  waiting for transfers between devices: 13.9 us -> 13 us
    all_to_all x1, starting transfers between devices: 4.67 us -> 3.51 us  [body(): lax.all_to_all(kept, 'wide', 0, 0, tiled=True, axis_index_groups=groups_z)]
    ppermute x16, waiting for transfers between devices: 12.5 us -> 11.3 us  [shifted(): lax.ppermute(x, axis, [(i, target(i)) for i in range(lax.axis_size(axis))])]
  transfers between devices with their start and end apart: 18 -> 18, of which waited for: 7 -> 7; matrix products, arithmetic and copies ran while one was open for 3% -> 3% of each run, Pallas kernels for 12% -> 13%
where the time goes in v3:
time: 65.8 us; the launch traced here: 65.6 us
  starting transfers between devices  33.7 us (51%)
  Pallas kernels  15.4 us (23%)
  waiting for transfers between devices  13 us (20%)
  other arithmetic  1.83 us (3%)
  matrix products  0.94 us (1%)
  between operations  0.75 us (1%)
    ppermute x16, starting transfers between devices, shifted(): lax.ppermute(x, axis, [(i, target(i)) for i in range(lax.axis_size(axis))])  25.4 us
    ppermute x16, waiting for transfers between devices, shifted(): lax.ppermute(x, axis, [(i, target(i)) for i in range(lax.axis_size(axis))])  11.3 us
    pallas_call x1, Pallas kernels, front(): pl.pallas_call(functools.partial(front_kernel, scale=1.0 / rows_total), o...  7.14 us
    pallas_call x1, Pallas kernels, factor(): pl.pallas_call(factor_kernel, out_shape=jax.ShapeDtypeStruct((order, orde...  6.53 us
    all_to_all x1, starting transfers between devices, body(): lax.all_to_all(kept, 'wide', 0, 0, tiled=True, axis_index_groups=groups_x)  4.8 us
    all_to_all x1, starting transfers between devices, body(): lax.all_to_all(kept, 'wide', 0, 0, tiled=True, axis_index_groups=groups_z)  3.51 us
    pallas_call x1, Pallas kernels, basis_of(): pl.pallas_call(basis_kernel, out_shape=jax.ShapeDtypeStruct((rows, order)...  1.71 us
    all_to_all x1, waiting for transfers between devices, body(): lax.all_to_all(kept, 'wide', 0, 0, tiled=True, axis_index_groups=groups_z)  1.65 us
  transfers between devices with their start and end apart: 18, of which 7 were waited for; matrix products, arithmetic and copies ran while one was open for 3% of the time, Pallas kernels for 13%

profile of v3, /device:TPU:4, one launch (start us, length us, event | category | flops | bytes accessed | tf_op | source)
XLA Modules:
  0.0 65.6 jit_solution(17884350061754345748)
XLA Ops:
  0.6 7.1 %shard_map.41 = (bf16[2048,256]{1,0:T(8,128)(2,1)}, f32[160,128]{1,0:T(8,128)S(1)}, f32[160,128]{1,0:T(8,128)S(1)}, f32[4,8,24,256]{3,2,1,0:T(8,128)S(1)}, f32[4,8,24,256]{3,2,1,0:T(8,128)S(1)}) custom-call(s32[1]{0:T(128)} %bitcast.core, bf16[2048,1536]{1,0:T(8,128)(2,1)} %e.1, bf16[1536,256]{1,0:T(8,128)(2,1)} %t.1), custom_call_target="tpu_custom_call" | custom-call | tf_op jit(solution)/shard_map/pallas_call | solution.py:282
  7.9 1.3 %collective-permute-done = f32[160,128]{1,0:T(8,128)S(1)} collective-permute-done((f32[160,128]{1,0:T(8,128)S(1)}, f32[160,128]{1,0:T(8,128)S(1)}, u32[]{:S(2)}, u32[]{:S(2)}) %collective-permute-start) | collective-permute-done | bytes 81952 | tf_op jit(solution)/shard_map/ppermute | solution.py:23
  9.4 1.9 %collective-permute-start.1 = (f32[160,128]{1,0:T(8,128)S(1)}, f32[160,128]{1,0:T(8,128)S(1)}, u32[]{:S(2)}, u32[]{:S(2)}) collective-permute-start(f32[160,128]{1,0:T(8,128)S(1)} %add.45), channel_id=1, source_target_pairs={{0,32},{4,36},{8,40},{12,44},{16,48},{20,52},{24,56},{28,60},{32,0... | collective-permute-start | bytes 245768 | tf_op jit(solution)/shard_map/ppermute | solution.py:23
  11.3 3.0 %collective-permute-done.1 = f32[160,128]{1,0:T(8,128)S(1)} collective-permute-done((f32[160,128]{1,0:T(8,128)S(1)}, f32[160,128]{1,0:T(8,128)S(1)}, u32[]{:S(2)}, u32[]{:S(2)}) %collective-permute-start.1) | collective-permute-done | bytes 81952 | tf_op jit(solution)/shard_map/ppermute | solution.py:23
  14.3 6.7 %collective-permute-start.4 = (f32[160,128]{1,0:T(8,128)S(1)}, f32[160,128]{1,0:T(8,128)S(1)}, u32[]{:S(2)}, u32[]{:S(2)}) collective-permute-start(f32[160,128]{1,0:T(8,128)S(1)} %add.46), channel_id=1, source_target_pairs={{0,160},{4,164},{8,168},{12,172},{16,176},{20,180},{24,184},{28,18... | collective-permute-start | bytes 245768 | tf_op jit(solution)/shard_map/ppermute | solution.py:23
  21.5 3.1 %collective-permute-start.2 = (f32[160,128]{1,0:T(8,128)S(1)}, f32[160,128]{1,0:T(8,128)S(1)}, u32[]{:S(2)}, u32[]{:S(2)}) collective-permute-start(f32[160,128]{1,0:T(8,128)S(1)} %add.46), channel_id=1, source_target_pairs={{0,224},{4,228},{8,232},{12,236},{16,240},{20,244},{24,248},{28,25... | collective-permute-start | bytes 245768 | tf_op jit(solution)/shard_map/ppermute | solution.py:23
  24.7 1.0 %add.56 = f32[4,8,24,256]{3,2,1,0:T(8,128)} add(f32[4,8,24,256]{3,2,1,0:T(8,128)S(1)} %get-tuple-element.16, f32[4,8,24,256]{3,2,1,0:T(8,128)S(1)} %collective-permute-done.12) | non-fusion elementwise | flops 196608 | bytes 2359296 | tf_op jit(solution)/shard_map/add | solution.py:317
  25.7 4.8 %all-to-all-start = ((f32[4,8,24,256]{3,2,1,0:T(8,128)}), f32[4,8,24,256]{3,2,1,0:T(8,128)S(1)}, u32[]{:S(2)}, u32[]{:S(2)}) async-start(f32[4,8,24,256]{3,2,1,0:T(8,128)} %add.56), calls=%async_computation | async-start | bytes 1572864 | tf_op jit(solution)/shard_map/all_to_all | solution.py:318
  30.5 3.1 %collective-permute-start.7 = (f32[160,128]{1,0:T(8,128)S(1)}, f32[160,128]{1,0:T(8,128)S(1)}, u32[]{:S(2)}, u32[]{:S(2)}) collective-permute-start(f32[160,128]{1,0:T(8,128)S(1)} %add_add_fusion.2), channel_id=1, source_target_pairs={{0,3},{1,2},{2,1},{3,0},{4,7},{5,6},{6,5},{7,4},{8,11},{9,10},{10,... | collective-permute-start | bytes 245768 | tf_op jit(solution)/shard_map/ppermute | solution.py:23
  34.7 2.4 %collective-permute-done.7 = f32[160,128]{1,0:T(8,128)S(1)} collective-permute-done((f32[160,128]{1,0:T(8,128)S(1)}, f32[160,128]{1,0:T(8,128)S(1)}, u32[]{:S(2)}, u32[]{:S(2)}) %collective-permute-start.7) | collective-permute-done | bytes 81952 | tf_op jit(solution)/shard_map/ppermute | solution.py:23
  37.1 2.4 %collective-permute-done.6 = f32[160,128]{1,0:T(8,128)S(1)} collective-permute-done((f32[160,128]{1,0:T(8,128)S(1)}, f32[160,128]{1,0:T(8,128)S(1)}, u32[]{:S(2)}, u32[]{:S(2)}) %collective-permute-start.6) | collective-permute-done | bytes 81952 | tf_op jit(solution)/shard_map/ppermute | solution.py:23
  40.2 2.7 %collective-permute-start.9 = (f32[160,128]{1,0:T(8,128)S(1)}, f32[160,128]{1,0:T(8,128)S(1)}, u32[]{:S(2)}, u32[]{:S(2)}) collective-permute-start(f32[160,128]{1,0:T(8,128)S(1)} %add_add_fusion.1), channel_id=1, source_target_pairs={{0,16},{4,20},{8,24},{12,28},{16,0},{20,4},{24,8},{28,12},{32,48},... | collective-permute-start | bytes 245768 | tf_op jit(solution)/shard_map/ppermute | solution.py:23
  42.9 0.9 %collective-permute-start.8 = (f32[160,128]{1,0:T(8,128)S(1)}, f32[160,128]{1,0:T(8,128)S(1)}, u32[]{:S(2)}, u32[]{:S(2)}) collective-permute-start(f32[160,128]{1,0:T(8,128)S(1)} %add_add_fusion.1), channel_id=1, source_target_pairs={{0,8},{4,12},{8,0},{12,4},{16,24},{20,28},{24,16},{28,20},{32,40},... | collective-permute-start | bytes 245768 | tf_op jit(solution)/shard_map/ppermute | solution.py:23
  43.8 0.7 %reduce_sum.18 = f32[8,24,256]{2,1,0:T(8,128)} reduce(f32[4,8,24,256]{3,2,1,0:T(8,128)S(1)} %all-to-all-done, f32[]{:T(128)} %constant.11.clone.1), dimensions={0}, to_apply=%region_0.0 | reduce | flops 147456 | bytes 983044 | tf_op jit(solution)/shard_map/reduce_sum | solution.py:322
  44.5 3.5 %all-to-all-start.1 = ((f32[8,24,256]{2,1,0:T(8,128)}), f32[8,24,256]{2,1,0:T(8,128)S(1)}, u32[]{:S(2)}, u32[]{:S(2)}) async-start(f32[8,24,256]{2,1,0:T(8,128)} %reduce_sum.18), calls=%async_computation.1 | async-start | bytes 393216 | tf_op jit(solution)/shard_map/all_to_all | solution.py:323
  48.3 1.3 %collective-permute-done.11.other = f32[160,128]{1,0:T(8,128)S(1)} collective-permute-done((f32[160,128]{1,0:T(8,128)S(1)}, f32[160,128]{1,0:T(8,128)S(1)}, u32[]{:S(2)}, u32[]{:S(2)}) %collective-permute-start.11) | collective-permute-done | bytes 81952 | tf_op jit(solution)/shard_map/ppermute | solution.py:23
  49.6 6.5 %shard_map.42.inv_t = f32[256,256]{1,0:T(8,128)S(1)} custom-call(s32[1]{0:T(128)} %bitcast.core, f32[160,128]{1,0:T(8,128)S(1)} %add_add_fusion.mine, f32[160,128]{1,0:T(8,128)S(1)} %collective-permute-done.11.other), custom_call_target="tpu_custom_call" | custom-call | bytes 20971520 | tf_op jit(solution)/shard_map/pallas_call | solution.py:163
  56.1 1.6 %all-to-all-done.1 = f32[8,24,256]{2,1,0:T(8,128)S(1)} async-done(((f32[8,24,256]{2,1,0:T(8,128)}), f32[8,24,256]{2,1,0:T(8,128)S(1)}, u32[]{:S(2)}, u32[]{:S(2)}) %all-to-all-start.1) | async-done | bytes 196640 | tf_op jit(solution)/shard_map/all_to_all | solution.py:323
  57.8 1.5 %collective-permute-start.15 = (f32[24,256]{1,0:T(8,128)S(1)}, f32[24,256]{1,0:T(8,128)S(1)}, u32[]{:S(2)}, u32[]{:S(2)}) collective-permute-start(f32[24,256]{1,0:T(8,128)S(1)} %reduce_sum.19), channel_id=1, source_target_pairs={{0,3},{1,2},{2,1},{3,0},{4,7},{5,6},{6,5},{7,4},{8,11},{9,10},{10,... | collective-permute-start | bytes 73736 | tf_op jit(solution)/shard_map/ppermute | solution.py:23
  59.3 0.8 %collective-permute-start.14 = (f32[24,256]{1,0:T(8,128)S(1)}, f32[24,256]{1,0:T(8,128)S(1)}, u32[]{:S(2)}, u32[]{:S(2)}) collective-permute-start(f32[24,256]{1,0:T(8,128)S(1)} %reduce_sum.19), channel_id=1, source_target_pairs={{0,2},{1,3},{2,0},{3,1},{4,6},{5,7},{6,4},{7,5},{8,10},{9,11},{10,... | collective-permute-start | bytes 73736 | tf_op jit(solution)/shard_map/ppermute | solution.py:23
  60.1 1.9 %collective-permute-start.13 = (f32[24,256]{1,0:T(8,128)S(1)}, f32[24,256]{1,0:T(8,128)S(1)}, u32[]{:S(2)}, u32[]{:S(2)}) collective-permute-start(f32[24,256]{1,0:T(8,128)S(1)} %reduce_sum.19), channel_id=1, source_target_pairs={{0,1},{1,0},{2,3},{3,2},{4,5},{5,4},{6,7},{7,6},{8,9},{9,8},{10,11... | collective-permute-start | bytes 73736 | tf_op jit(solution)/shard_map/ppermute | solution.py:23
  62.0 1.7 %shard_map.43 = f32[2048,256]{1,0:T(8,128)} custom-call(bf16[2048,256]{1,0:T(8,128)(2,1)S(1)} %copy-done, f32[256,256]{1,0:T(8,128)S(1)} %shard_map.42.inv_t), custom_call_target="tpu_custom_call" | custom-call | flops 536870912 | bytes 3145728 | tf_op jit(solution)/shard_map/pallas_call | solution.py:198
  63.7 0.9 %collective-permute-done.14 = f32[24,256]{1,0:T(8,128)S(1)} collective-permute-done((f32[24,256]{1,0:T(8,128)S(1)}, f32[24,256]{1,0:T(8,128)S(1)}, u32[]{:S(2)}, u32[]{:S(2)}) %collective-permute-start.14) | collective-permute-done | bytes 24608 | tf_op jit(solution)/shard_map/ppermute | solution.py:23
  64.6 0.9 %convolution_multiply_fusion = f32[24,256]{1,0:T(8,128)} fusion(f32[256,256]{1,0:T(8,128)S(1)} %shard_map.42.inv_t, f32[24,256]{1,0:T(8,128)S(1)} %collective-permute-done.14, f32[24,256]{1,0:T(8,128)S(1)} %collective-permute-done.15, f32[24,256]{1,0:T(8,128)S(1)} %reduce_sum.19, f32[24,256]{1,0:T(8,128)S(1)} %collective-permute-done.13), kind=kOutput, calls=%fused_computation | convolution fusion | flops 18898944 | bytes 385024 | tf_op jit(solution)/shard_map/dot_general | solution.py:336
  (26 shorter events, 3.0 us)
Async XLA Ops:
  7.8 54.2 %copy-start = (bf16[2048,256]{1,0:T(8,128)(2,1)S(1)}, bf16[2048,256]{1,0:T(8,128)(2,1)}, u32[]{:S(2)}) copy-start(bf16[2048,256]{1,0:T(8,128)(2,1)} %get-tuple-element.11.sketch) | copy-start | bytes 3145732
  7.8 1.4 %collective-permute-start = (f32[160,128]{1,0:T(8,128)S(1)}, f32[160,128]{1,0:T(8,128)S(1)}, u32[]{:S(2)}, u32[]{:S(2)}) collective-permute-start(f32[160,128]{1,0:T(8,128)S(1)} %get-tuple-element.13), channel_id=1, source_target_pairs={{0,4},{4,0},{8,12},{12,8},{16,20},{20,16},{24,28},{28,24},{32,36},... | collective-permute-start | bytes 245768 | tf_op jit(solution)/shard_map/ppermute | solution.py:23
  9.2 15.5 %collective-permute-start.12 = (f32[4,8,24,256]{3,2,1,0:T(8,128)S(1)}, f32[4,8,24,256]{3,2,1,0:T(8,128)S(1)}, u32[]{:S(2)}, u32[]{:S(2)}) collective-permute-start(f32[4,8,24,256]{3,2,1,0:T(8,128)S(1)} %get-tuple-element.17), channel_id=1, source_target_pairs={{0,4},{4,0},{8,12},{12,8},{16,20},{20,16},{24,28},{28,24},{32,36},... | collective-permute-start | bytes 2359304 | tf_op jit(solution)/shard_map/ppermute | solution.py:23
  9.4 4.9 %collective-permute-start.1 = (f32[160,128]{1,0:T(8,128)S(1)}, f32[160,128]{1,0:T(8,128)S(1)}, u32[]{:S(2)}, u32[]{:S(2)}) collective-permute-start(f32[160,128]{1,0:T(8,128)S(1)} %add.45), channel_id=1, source_target_pairs={{0,32},{4,36},{8,40},{12,44},{16,48},{20,52},{24,56},{28,60},{32,0... | collective-permute-start | bytes 245768 | tf_op jit(solution)/shard_map/ppermute | solution.py:23
  14.3 16.1 %collective-permute-start.4 = (f32[160,128]{1,0:T(8,128)S(1)}, f32[160,128]{1,0:T(8,128)S(1)}, u32[]{:S(2)}, u32[]{:S(2)}) collective-permute-start(f32[160,128]{1,0:T(8,128)S(1)} %add.46), channel_id=1, source_target_pairs={{0,160},{4,164},{8,168},{12,172},{16,176},{20,180},{24,184},{28,18... | collective-permute-start | bytes 245768 | tf_op jit(solution)/shard_map/ppermute | solution.py:23
  21.0 9.5 %collective-permute-start.3 = (f32[160,128]{1,0:T(8,128)S(1)}, f32[160,128]{1,0:T(8,128)S(1)}, u32[]{:S(2)}, u32[]{:S(2)}) collective-permute-start(f32[160,128]{1,0:T(8,128)S(1)} %add.46), channel_id=1, source_target_pairs={{0,192},{4,196},{8,200},{12,204},{16,208},{20,212},{24,216},{28,22... | collective-permute-start | bytes 245768 | tf_op jit(solution)/shard_map/ppermute | solution.py:23
  21.5 8.9 %collective-permute-start.2 = (f32[160,128]{1,0:T(8,128)S(1)}, f32[160,128]{1,0:T(8,128)S(1)}, u32[]{:S(2)}, u32[]{:S(2)}) collective-permute-start(f32[160,128]{1,0:T(8,128)S(1)} %add.46), channel_id=1, source_target_pairs={{0,224},{4,228},{8,232},{12,236},{16,240},{20,244},{24,248},{28,25... | collective-permute-start | bytes 245768 | tf_op jit(solution)/shard_map/ppermute | solution.py:23
  25.7 18.1 %all-to-all-start = ((f32[4,8,24,256]{3,2,1,0:T(8,128)}), f32[4,8,24,256]{3,2,1,0:T(8,128)S(1)}, u32[]{:S(2)}, u32[]{:S(2)}) async-start(f32[4,8,24,256]{3,2,1,0:T(8,128)} %add.56), calls=%async_computation | async-start | bytes 1572864 | tf_op jit(solution)/shard_map/all_to_all | solution.py:318
  30.5 6.6 %collective-permute-start.7 = (f32[160,128]{1,0:T(8,128)S(1)}, f32[160,128]{1,0:T(8,128)S(1)}, u32[]{:S(2)}, u32[]{:S(2)}) collective-permute-start(f32[160,128]{1,0:T(8,128)S(1)} %add_add_fusion.2), channel_id=1, source_target_pairs={{0,3},{1,2},{2,1},{3,0},{4,7},{5,6},{6,5},{7,4},{8,11},{9,10},{10,... | collective-permute-start | bytes 245768 | tf_op jit(solution)/shard_map/ppermute | solution.py:23
  33.6 5.9 %collective-permute-start.6 = (f32[160,128]{1,0:T(8,128)S(1)}, f32[160,128]{1,0:T(8,128)S(1)}, u32[]{:S(2)}, u32[]{:S(2)}) collective-permute-start(f32[160,128]{1,0:T(8,128)S(1)} %add_add_fusion.2), channel_id=1, source_target_pairs={{0,2},{1,3},{2,0},{3,1},{4,6},{5,7},{6,4},{7,5},{8,10},{9,11},{10,... | collective-permute-start | bytes 245768 | tf_op jit(solution)/shard_map/ppermute | solution.py:23
  34.2 5.3 %collective-permute-start.5 = (f32[160,128]{1,0:T(8,128)S(1)}, f32[160,128]{1,0:T(8,128)S(1)}, u32[]{:S(2)}, u32[]{:S(2)}) collective-permute-start(f32[160,128]{1,0:T(8,128)S(1)} %add_add_fusion.2), channel_id=1, source_target_pairs={{0,1},{1,0},{2,3},{3,2},{4,5},{5,4},{6,7},{7,6},{8,9},{9,8},{10,11... | collective-permute-start | bytes 245768 | tf_op jit(solution)/shard_map/ppermute | solution.py:23
  39.6 8.4 %collective-permute-start.10 = (f32[160,128]{1,0:T(8,128)S(1)}, f32[160,128]{1,0:T(8,128)S(1)}, u32[]{:S(2)}, u32[]{:S(2)}) collective-permute-start(f32[160,128]{1,0:T(8,128)S(1)} %add_add_fusion.1), channel_id=1, source_target_pairs={{0,24},{4,28},{8,16},{12,20},{16,8},{20,12},{24,0},{28,4},{32,56},... | collective-permute-start | bytes 245768 | tf_op jit(solution)/shard_map/ppermute | solution.py:23
  40.2 7.8 %collective-permute-start.9 = (f32[160,128]{1,0:T(8,128)S(1)}, f32[160,128]{1,0:T(8,128)S(1)}, u32[]{:S(2)}, u32[]{:S(2)}) collective-permute-start(f32[160,128]{1,0:T(8,128)S(1)} %add_add_fusion.1), channel_id=1, source_target_pairs={{0,16},{4,20},{8,24},{12,28},{16,0},{20,4},{24,8},{28,12},{32,48},... | collective-permute-start | bytes 245768 | tf_op jit(solution)/shard_map/ppermute | solution.py:23
  42.9 5.1 %collective-permute-start.8 = (f32[160,128]{1,0:T(8,128)S(1)}, f32[160,128]{1,0:T(8,128)S(1)}, u32[]{:S(2)}, u32[]{:S(2)}) collective-permute-start(f32[160,128]{1,0:T(8,128)S(1)} %add_add_fusion.1), channel_id=1, source_target_pairs={{0,8},{4,12},{8,0},{12,4},{16,24},{20,28},{24,16},{28,20},{32,40},... | collective-permute-start | bytes 245768 | tf_op jit(solution)/shard_map/ppermute | solution.py:23
  44.5 13.3 %all-to-all-start.1 = ((f32[8,24,256]{2,1,0:T(8,128)}), f32[8,24,256]{2,1,0:T(8,128)S(1)}, u32[]{:S(2)}, u32[]{:S(2)}) async-start(f32[8,24,256]{2,1,0:T(8,128)} %reduce_sum.18), calls=%async_computation.1 | async-start | bytes 393216 | tf_op jit(solution)/shard_map/all_to_all | solution.py:323
  48.0 1.5 %collective-permute-start.11 = (f32[160,128]{1,0:T(8,128)S(1)}, f32[160,128]{1,0:T(8,128)S(1)}, u32[]{:S(2)}, u32[]{:S(2)}) collective-permute-start(f32[160,128]{1,0:T(8,128)S(1)} %add_add_fusion.mine), channel_id=1, source_target_pairs={{0,4},{4,0},{8,12},{12,8},{16,20},{20,16},{24,28},{28,24},{32,36},... | collective-permute-start | bytes 245768 | tf_op jit(solution)/shard_map/ppermute | solution.py:23
  57.8 5.9 %collective-permute-start.15 = (f32[24,256]{1,0:T(8,128)S(1)}, f32[24,256]{1,0:T(8,128)S(1)}, u32[]{:S(2)}, u32[]{:S(2)}) collective-permute-start(f32[24,256]{1,0:T(8,128)S(1)} %reduce_sum.19), channel_id=1, source_target_pairs={{0,3},{1,2},{2,1},{3,0},{4,7},{5,6},{6,5},{7,4},{8,11},{9,10},{10,... | collective-permute-start | bytes 73736 | tf_op jit(solution)/shard_map/ppermute | solution.py:23
  59.3 5.3 %collective-permute-start.14 = (f32[24,256]{1,0:T(8,128)S(1)}, f32[24,256]{1,0:T(8,128)S(1)}, u32[]{:S(2)}, u32[]{:S(2)}) collective-permute-start(f32[24,256]{1,0:T(8,128)S(1)} %reduce_sum.19), channel_id=1, source_target_pairs={{0,2},{1,3},{2,0},{3,1},{4,6},{5,7},{6,4},{7,5},{8,10},{9,11},{10,... | collective-permute-start | bytes 73736 | tf_op jit(solution)/shard_map/ppermute | solution.py:23
  60.1 4.6 %collective-permute-start.13 = (f32[24,256]{1,0:T(8,128)S(1)}, f32[24,256]{1,0:T(8,128)S(1)}, u32[]{:S(2)}, u32[]{:S(2)}) collective-permute-start(f32[24,256]{1,0:T(8,128)S(1)} %reduce_sum.19), channel_id=1, source_target_pairs={{0,1},{1,0},{2,3},{3,2},{4,5},{5,4},{6,7},{7,6},{8,9},{9,8},{10,11... | collective-permute-start | bytes 73736 | tf_op jit(solution)/shard_map/ppermute | solution.py:23

commit v4 on v3

--- a/solution.py
+++ b/solution.py
@@ -93,15 +93,17 @@
             for i in range(0, SUB, 2):
                 j = i + 1
                 a, b, c = splat(cols[i], sub=i), splat(cols[i], sub=j), splat(cols[j], sub=j)
-                inv_det, inv_a = 1.0 / (a * c - b * b), 1.0 / a
+                inv_a = 1.0 / a
+                ratio = b * inv_a
+                inv_c = 1.0 / (c - b * ratio)
                 pair = (row == i) | (row == j)
                 ci = jnp.where(row == i, -1.0, jnp.where(row == j, 0.0, cols[i]))
                 cj = jnp.where(row == j, -1.0, jnp.where(row == i, 0.0, cols[j]))
-                mi = (ci * c - cj * b) * inv_det
-                mj = (cj * a - ci * b) * inv_det
-                fi = jnp.where(row > j, mi, jnp.where(row == j, b * inv_a, 0.0))
+                mj = (cj - ci * ratio) * inv_c
+                mi = ci * inv_a - mj * ratio
+                fi = jnp.where(row > j, mi, jnp.where(row == j, ratio, 0.0))
                 fj = jnp.where(row > j, mj, 0.0)
-                inv_d = jnp.where(row == i, inv_a, jnp.where(row == j, a * inv_det, inv_d))
+                inv_d = jnp.where(row == i, inv_a, jnp.where(row == j, inv_c, inv_d))
 
                 def eliminated(x):
                     x_i, x_j = splat(x, sub=i), splat(x, sub=j)
@@ -299,16 +301,11 @@
     )(core, e, t)
 
 
-def pick(x, index):
-    return lax.dynamic_index_in_dim(x, index, 0, keepdims=False)
-
-
 def body(embeddings, test_matrix):
     n_wide = lax.axis_size("wide")
     rows_total = embeddings.shape[0] * n_wide * lax.axis_size("narrow")
     place = lax.axis_index("wide")
-    core, x_at, z_at = place & 1, place >> 1 & 3, place >> 3
-    at = core.reshape(1)
+    at = (place & 1).reshape(1)
     sketch, mine, theirs, kept, given = front(at, embeddings, test_matrix, rows_total, 4, 8)
     groups_x = [[z * 8 + x * 2 + c for x in range(4)] for z in range(8) for c in range(2)]
     groups_z = [[z * 8 + r for z in range(8)] for r in range(8)]
@@ -341,9 +338,6 @@
     return (basis_rows, loadings)
 
 
-CROSS = "a2a"
-
-
 def solution(mesh):
     in_specs = (P(("wide", "narrow"), None), P())
     out_specs = (P(("wide", "narrow"), None), P("wide", None))

time: 65.8 us -> 65.8 us (level)
  Pallas kernels: 15.4 us -> 16.5 us
  waiting for transfers between devices: 13 us -> 11.9 us
    all_to_all x1, waiting for transfers between devices: 1.65 us -> 0.56 us  [body(): lax.all_to_all(kept, 'wide', 0, 0, tiled=True, axis_index_groups=groups_z)]
    pallas_call x1, Pallas kernels: 6.53 us -> 7.61 us  [factor(): pl.pallas_call(factor_kernel, out_shape=jax.ShapeDtypeStruct((order, orde...]
  transfers between devices with their start and end apart: 18 -> 18, of which waited for: 7 -> 7; matrix products, arithmetic and copies ran while one was open for 3% -> 3% of each run, Pallas kernels for 13% -> 14%
where the time goes in v4:
time: 65.8 us; the launch traced here: 65.6 us
  starting transfers between devices  33.7 us (51%)
  Pallas kernels  16.5 us (25%)
  waiting for transfers between devices  11.9 us (18%)
  other arithmetic  1.83 us (3%)
  matrix products  0.94 us (1%)
  between operations  0.76 us (1%)
    ppermute x16, starting transfers between devices, shifted(): lax.ppermute(x, axis, [(i, target(i)) for i in range(lax.axis_size(axis))])  25.4 us
    ppermute x16, waiting for transfers between devices, shifted(): lax.ppermute(x, axis, [(i, target(i)) for i in range(lax.axis_size(axis))])  11.3 us
    pallas_call x1, Pallas kernels, factor(): pl.pallas_call(factor_kernel, out_shape=jax.ShapeDtypeStruct((order, orde...  7.61 us
    pallas_call x1, Pallas kernels, front(): pl.pallas_call(functools.partial(front_kernel, scale=1.0 / rows_total), o...  7.14 us
    all_to_all x1, starting transfers between devices, body(): lax.all_to_all(kept, 'wide', 0, 0, tiled=True, axis_index_groups=groups_x)  4.8 us
    all_to_all x1, starting transfers between devices, body(): lax.all_to_all(kept, 'wide', 0, 0, tiled=True, axis_index_groups=groups_z)  3.51 us
    pallas_call x1, Pallas kernels, basis_of(): pl.pallas_call(basis_kernel, out_shape=jax.ShapeDtypeStruct((rows, order)...  1.71 us
  transfers between devices with their start and end apart: 18, of which 7 were waited for; matrix products, arithmetic and copies ran while one was open for 3% of the time, Pallas kernels for 14%

profile of v4, /device:TPU:4, one launch (start us, length us, event | category | flops | bytes accessed | tf_op | source)
XLA Modules:
  0.0 65.6 jit_solution(8979184219775151775)
XLA Ops:
  0.6 7.1 %shard_map.41 = (bf16[2048,256]{1,0:T(8,128)(2,1)}, f32[160,128]{1,0:T(8,128)S(1)}, f32[160,128]{1,0:T(8,128)S(1)}, f32[4,8,24,256]{3,2,1,0:T(8,128)S(1)}, f32[4,8,24,256]{3,2,1,0:T(8,128)S(1)}) custom-call(s32[1]{0:T(128)} %bitcast.core, bf16[2048,1536]{1,0:T(8,128)(2,1)} %e.1, bf16[1536,256]{1,0:T(8,128)(2,1)} %t.1), custom_call_target="tpu_custom_call" | custom-call | tf_op jit(solution)/shard_map/pallas_call | solution.py:284
  7.9 1.3 %collective-permute-done = f32[160,128]{1,0:T(8,128)S(1)} collective-permute-done((f32[160,128]{1,0:T(8,128)S(1)}, f32[160,128]{1,0:T(8,128)S(1)}, u32[]{:S(2)}, u32[]{:S(2)}) %collective-permute-start) | collective-permute-done | bytes 81952 | tf_op jit(solution)/shard_map/ppermute | solution.py:23
  9.4 1.9 %collective-permute-start.1 = (f32[160,128]{1,0:T(8,128)S(1)}, f32[160,128]{1,0:T(8,128)S(1)}, u32[]{:S(2)}, u32[]{:S(2)}) collective-permute-start(f32[160,128]{1,0:T(8,128)S(1)} %add.45), channel_id=1, source_target_pairs={{0,32},{4,36},{8,40},{12,44},{16,48},{20,52},{24,56},{28,60},{32,0... | collective-permute-start | bytes 245768 | tf_op jit(solution)/shard_map/ppermute | solution.py:23
  11.3 3.0 %collective-permute-done.1 = f32[160,128]{1,0:T(8,128)S(1)} collective-permute-done((f32[160,128]{1,0:T(8,128)S(1)}, f32[160,128]{1,0:T(8,128)S(1)}, u32[]{:S(2)}, u32[]{:S(2)}) %collective-permute-start.1) | collective-permute-done | bytes 81952 | tf_op jit(solution)/shard_map/ppermute | solution.py:23
  14.3 6.7 %collective-permute-start.4 = (f32[160,128]{1,0:T(8,128)S(1)}, f32[160,128]{1,0:T(8,128)S(1)}, u32[]{:S(2)}, u32[]{:S(2)}) collective-permute-start(f32[160,128]{1,0:T(8,128)S(1)} %add.46), channel_id=1, source_target_pairs={{0,160},{4,164},{8,168},{12,172},{16,176},{20,180},{24,184},{28,18... | collective-permute-start | bytes 245768 | tf_op jit(solution)/shard_map/ppermute | solution.py:23
  21.5 3.1 %collective-permute-start.2 = (f32[160,128]{1,0:T(8,128)S(1)}, f32[160,128]{1,0:T(8,128)S(1)}, u32[]{:S(2)}, u32[]{:S(2)}) collective-permute-start(f32[160,128]{1,0:T(8,128)S(1)} %add.46), channel_id=1, source_target_pairs={{0,224},{4,228},{8,232},{12,236},{16,240},{20,244},{24,248},{28,25... | collective-permute-start | bytes 245768 | tf_op jit(solution)/shard_map/ppermute | solution.py:23
  24.7 1.0 %add.56 = f32[4,8,24,256]{3,2,1,0:T(8,128)} add(f32[4,8,24,256]{3,2,1,0:T(8,128)S(1)} %get-tuple-element.16, f32[4,8,24,256]{3,2,1,0:T(8,128)S(1)} %collective-permute-done.12) | non-fusion elementwise | flops 196608 | bytes 2359296 | tf_op jit(solution)/shard_map/add | solution.py:314
  25.7 4.8 %all-to-all-start = ((f32[4,8,24,256]{3,2,1,0:T(8,128)}), f32[4,8,24,256]{3,2,1,0:T(8,128)S(1)}, u32[]{:S(2)}, u32[]{:S(2)}) async-start(f32[4,8,24,256]{3,2,1,0:T(8,128)} %add.56), calls=%async_computation | async-start | bytes 1572864 | tf_op jit(solution)/shard_map/all_to_all | solution.py:315
  30.5 3.1 %collective-permute-start.7 = (f32[160,128]{1,0:T(8,128)S(1)}, f32[160,128]{1,0:T(8,128)S(1)}, u32[]{:S(2)}, u32[]{:S(2)}) collective-permute-start(f32[160,128]{1,0:T(8,128)S(1)} %add_add_fusion.2), channel_id=1, source_target_pairs={{0,3},{1,2},{2,1},{3,0},{4,7},{5,6},{6,5},{7,4},{8,11},{9,10},{10,... | collective-permute-start | bytes 245768 | tf_op jit(solution)/shard_map/ppermute | solution.py:23
  34.7 2.4 %collective-permute-done.7 = f32[160,128]{1,0:T(8,128)S(1)} collective-permute-done((f32[160,128]{1,0:T(8,128)S(1)}, f32[160,128]{1,0:T(8,128)S(1)}, u32[]{:S(2)}, u32[]{:S(2)}) %collective-permute-start.7) | collective-permute-done | bytes 81952 | tf_op jit(solution)/shard_map/ppermute | solution.py:23
  37.1 2.4 %collective-permute-done.6 = f32[160,128]{1,0:T(8,128)S(1)} collective-permute-done((f32[160,128]{1,0:T(8,128)S(1)}, f32[160,128]{1,0:T(8,128)S(1)}, u32[]{:S(2)}, u32[]{:S(2)}) %collective-permute-start.6) | collective-permute-done | bytes 81952 | tf_op jit(solution)/shard_map/ppermute | solution.py:23
  39.6 0.6 collective-permute-start.10
  40.2 2.7 %collective-permute-start.9 = (f32[160,128]{1,0:T(8,128)S(1)}, f32[160,128]{1,0:T(8,128)S(1)}, u32[]{:S(2)}, u32[]{:S(2)}) collective-permute-start(f32[160,128]{1,0:T(8,128)S(1)} %add_add_fusion.1), channel_id=1, source_target_pairs={{0,16},{4,20},{8,24},{12,28},{16,0},{20,4},{24,8},{28,12},{32,48},... | collective-permute-start | bytes 245768 | tf_op jit(solution)/shard_map/ppermute | solution.py:23
  42.9 0.9 %collective-permute-start.8 = (f32[160,128]{1,0:T(8,128)S(1)}, f32[160,128]{1,0:T(8,128)S(1)}, u32[]{:S(2)}, u32[]{:S(2)}) collective-permute-start(f32[160,128]{1,0:T(8,128)S(1)} %add_add_fusion.1), channel_id=1, source_target_pairs={{0,8},{4,12},{8,0},{12,4},{16,24},{20,28},{24,16},{28,20},{32,40},... | collective-permute-start | bytes 245768 | tf_op jit(solution)/shard_map/ppermute | solution.py:23
  43.8 0.7 %reduce_sum.18 = f32[8,24,256]{2,1,0:T(8,128)} reduce(f32[4,8,24,256]{3,2,1,0:T(8,128)S(1)} %all-to-all-done, f32[]{:T(128)} %constant.11.clone.1), dimensions={0}, to_apply=%region_0.0 | reduce | flops 147456 | bytes 983044 | tf_op jit(solution)/shard_map/reduce_sum | solution.py:319
  44.5 3.5 %all-to-all-start.1 = ((f32[8,24,256]{2,1,0:T(8,128)}), f32[8,24,256]{2,1,0:T(8,128)S(1)}, u32[]{:S(2)}, u32[]{:S(2)}) async-start(f32[8,24,256]{2,1,0:T(8,128)} %reduce_sum.18), calls=%async_computation.1 | async-start | bytes 393216 | tf_op jit(solution)/shard_map/all_to_all | solution.py:320
  48.3 1.3 %collective-permute-done.11.other = f32[160,128]{1,0:T(8,128)S(1)} collective-permute-done((f32[160,128]{1,0:T(8,128)S(1)}, f32[160,128]{1,0:T(8,128)S(1)}, u32[]{:S(2)}, u32[]{:S(2)}) %collective-permute-start.11) | collective-permute-done | bytes 81952 | tf_op jit(solution)/shard_map/ppermute | solution.py:23
  49.6 7.6 %shard_map.42.inv_t = f32[256,256]{1,0:T(8,128)S(1)} custom-call(s32[1]{0:T(128)} %bitcast.core, f32[160,128]{1,0:T(8,128)S(1)} %add_add_fusion.mine, f32[160,128]{1,0:T(8,128)S(1)} %collective-permute-done.11.other), custom_call_target="tpu_custom_call" | custom-call | bytes 20971520 | tf_op jit(solution)/shard_map/pallas_call | solution.py:165
  57.8 1.5 %collective-permute-start.15 = (f32[24,256]{1,0:T(8,128)S(1)}, f32[24,256]{1,0:T(8,128)S(1)}, u32[]{:S(2)}, u32[]{:S(2)}) collective-permute-start(f32[24,256]{1,0:T(8,128)S(1)} %reduce_sum.19), channel_id=1, source_target_pairs={{0,3},{1,2},{2,1},{3,0},{4,7},{5,6},{6,5},{7,4},{8,11},{9,10},{10,... | collective-permute-start | bytes 73736 | tf_op jit(solution)/shard_map/ppermute | solution.py:23
  59.3 0.8 %collective-permute-start.14 = (f32[24,256]{1,0:T(8,128)S(1)}, f32[24,256]{1,0:T(8,128)S(1)}, u32[]{:S(2)}, u32[]{:S(2)}) collective-permute-start(f32[24,256]{1,0:T(8,128)S(1)} %reduce_sum.19), channel_id=1, source_target_pairs={{0,2},{1,3},{2,0},{3,1},{4,6},{5,7},{6,4},{7,5},{8,10},{9,11},{10,... | collective-permute-start | bytes 73736 | tf_op jit(solution)/shard_map/ppermute | solution.py:23
  60.1 1.9 %collective-permute-start.13 = (f32[24,256]{1,0:T(8,128)S(1)}, f32[24,256]{1,0:T(8,128)S(1)}, u32[]{:S(2)}, u32[]{:S(2)}) collective-permute-start(f32[24,256]{1,0:T(8,128)S(1)} %reduce_sum.19), channel_id=1, source_target_pairs={{0,1},{1,0},{2,3},{3,2},{4,5},{5,4},{6,7},{7,6},{8,9},{9,8},{10,11... | collective-permute-start | bytes 73736 | tf_op jit(solution)/shard_map/ppermute | solution.py:23
  62.0 1.7 %shard_map.43 = f32[2048,256]{1,0:T(8,128)} custom-call(bf16[2048,256]{1,0:T(8,128)(2,1)S(1)} %copy-done, f32[256,256]{1,0:T(8,128)S(1)} %shard_map.42.inv_t), custom_call_target="tpu_custom_call" | custom-call | flops 536870912 | bytes 3145728 | tf_op jit(solution)/shard_map/pallas_call | solution.py:200
  63.7 0.9 %collective-permute-done.14 = f32[24,256]{1,0:T(8,128)S(1)} collective-permute-done((f32[24,256]{1,0:T(8,128)S(1)}, f32[24,256]{1,0:T(8,128)S(1)}, u32[]{:S(2)}, u32[]{:S(2)}) %collective-permute-start.14) | collective-permute-done | bytes 24608 | tf_op jit(solution)/shard_map/ppermute | solution.py:23
  64.6 0.9 %convolution_multiply_fusion = f32[24,256]{1,0:T(8,128)} fusion(f32[256,256]{1,0:T(8,128)S(1)} %shard_map.42.inv_t, f32[24,256]{1,0:T(8,128)S(1)} %collective-permute-done.14, f32[24,256]{1,0:T(8,128)S(1)} %collective-permute-done.15, f32[24,256]{1,0:T(8,128)S(1)} %reduce_sum.19, f32[24,256]{1,0:T(8,128)S(1)} %collective-permute-done.13), kind=kOutput, calls=%fused_computation | convolution fusion | flops 18898944 | bytes 385024 | tf_op jit(solution)/shard_map/dot_general | solution.py:333
  (26 shorter events, 2.9 us)
Async XLA Ops:
  7.8 54.2 %copy-start = (bf16[2048,256]{1,0:T(8,128)(2,1)S(1)}, bf16[2048,256]{1,0:T(8,128)(2,1)}, u32[]{:S(2)}) copy-start(bf16[2048,256]{1,0:T(8,128)(2,1)} %get-tuple-element.11.sketch) | copy-start | bytes 3145732
  7.8 1.4 %collective-permute-start = (f32[160,128]{1,0:T(8,128)S(1)}, f32[160,128]{1,0:T(8,128)S(1)}, u32[]{:S(2)}, u32[]{:S(2)}) collective-permute-start(f32[160,128]{1,0:T(8,128)S(1)} %get-tuple-element.13), channel_id=1, source_target_pairs={{0,4},{4,0},{8,12},{12,8},{16,20},{20,16},{24,28},{28,24},{32,36},... | collective-permute-start | bytes 245768 | tf_op jit(solution)/shard_map/ppermute | solution.py:23
  9.2 15.5 %collective-permute-start.12 = (f32[4,8,24,256]{3,2,1,0:T(8,128)S(1)}, f32[4,8,24,256]{3,2,1,0:T(8,128)S(1)}, u32[]{:S(2)}, u32[]{:S(2)}) collective-permute-start(f32[4,8,24,256]{3,2,1,0:T(8,128)S(1)} %get-tuple-element.17), channel_id=1, source_target_pairs={{0,4},{4,0},{8,12},{12,8},{16,20},{20,16},{24,28},{28,24},{32,36},... | collective-permute-start | bytes 2359304 | tf_op jit(solution)/shard_map/ppermute | solution.py:23
  9.4 4.9 %collective-permute-start.1 = (f32[160,128]{1,0:T(8,128)S(1)}, f32[160,128]{1,0:T(8,128)S(1)}, u32[]{:S(2)}, u32[]{:S(2)}) collective-permute-start(f32[160,128]{1,0:T(8,128)S(1)} %add.45), channel_id=1, source_target_pairs={{0,32},{4,36},{8,40},{12,44},{16,48},{20,52},{24,56},{28,60},{32,0... | collective-permute-start | bytes 245768 | tf_op jit(solution)/shard_map/ppermute | solution.py:23
  14.3 16.1 %collective-permute-start.4 = (f32[160,128]{1,0:T(8,128)S(1)}, f32[160,128]{1,0:T(8,128)S(1)}, u32[]{:S(2)}, u32[]{:S(2)}) collective-permute-start(f32[160,128]{1,0:T(8,128)S(1)} %add.46), channel_id=1, source_target_pairs={{0,160},{4,164},{8,168},{12,172},{16,176},{20,180},{24,184},{28,18... | collective-permute-start | bytes 245768 | tf_op jit(solution)/shard_map/ppermute | solution.py:23
  21.0 9.5 %collective-permute-start.3 = (f32[160,128]{1,0:T(8,128)S(1)}, f32[160,128]{1,0:T(8,128)S(1)}, u32[]{:S(2)}, u32[]{:S(2)}) collective-permute-start(f32[160,128]{1,0:T(8,128)S(1)} %add.46), channel_id=1, source_target_pairs={{0,192},{4,196},{8,200},{12,204},{16,208},{20,212},{24,216},{28,22... | collective-permute-start | bytes 245768 | tf_op jit(solution)/shard_map/ppermute | solution.py:23
  21.5 8.9 %collective-permute-start.2 = (f32[160,128]{1,0:T(8,128)S(1)}, f32[160,128]{1,0:T(8,128)S(1)}, u32[]{:S(2)}, u32[]{:S(2)}) collective-permute-start(f32[160,128]{1,0:T(8,128)S(1)} %add.46), channel_id=1, source_target_pairs={{0,224},{4,228},{8,232},{12,236},{16,240},{20,244},{24,248},{28,25... | collective-permute-start | bytes 245768 | tf_op jit(solution)/shard_map/ppermute | solution.py:23
  25.7 18.1 %all-to-all-start = ((f32[4,8,24,256]{3,2,1,0:T(8,128)}), f32[4,8,24,256]{3,2,1,0:T(8,128)S(1)}, u32[]{:S(2)}, u32[]{:S(2)}) async-start(f32[4,8,24,256]{3,2,1,0:T(8,128)} %add.56), calls=%async_computation | async-start | bytes 1572864 | tf_op jit(solution)/shard_map/all_to_all | solution.py:315
  30.5 6.6 %collective-permute-start.7 = (f32[160,128]{1,0:T(8,128)S(1)}, f32[160,128]{1,0:T(8,128)S(1)}, u32[]{:S(2)}, u32[]{:S(2)}) collective-permute-start(f32[160,128]{1,0:T(8,128)S(1)} %add_add_fusion.2), channel_id=1, source_target_pairs={{0,3},{1,2},{2,1},{3,0},{4,7},{5,6},{6,5},{7,4},{8,11},{9,10},{10,... | collective-permute-start | bytes 245768 | tf_op jit(solution)/shard_map/ppermute | solution.py:23
  33.6 5.9 %collective-permute-start.6 = (f32[160,128]{1,0:T(8,128)S(1)}, f32[160,128]{1,0:T(8,128)S(1)}, u32[]{:S(2)}, u32[]{:S(2)}) collective-permute-start(f32[160,128]{1,0:T(8,128)S(1)} %add_add_fusion.2), channel_id=1, source_target_pairs={{0,2},{1,3},{2,0},{3,1},{4,6},{5,7},{6,4},{7,5},{8,10},{9,11},{10,... | collective-permute-start | bytes 245768 | tf_op jit(solution)/shard_map/ppermute | solution.py:23
  34.2 5.3 %collective-permute-start.5 = (f32[160,128]{1,0:T(8,128)S(1)}, f32[160,128]{1,0:T(8,128)S(1)}, u32[]{:S(2)}, u32[]{:S(2)}) collective-permute-start(f32[160,128]{1,0:T(8,128)S(1)} %add_add_fusion.2), channel_id=1, source_target_pairs={{0,1},{1,0},{2,3},{3,2},{4,5},{5,4},{6,7},{7,6},{8,9},{9,8},{10,11... | collective-permute-start | bytes 245768 | tf_op jit(solution)/shard_map/ppermute | solution.py:23
  39.6 8.4 %collective-permute-start.10 = (f32[160,128]{1,0:T(8,128)S(1)}, f32[160,128]{1,0:T(8,128)S(1)}, u32[]{:S(2)}, u32[]{:S(2)}) collective-permute-start(f32[160,128]{1,0:T(8,128)S(1)} %add_add_fusion.1), channel_id=1, source_target_pairs={{0,24},{4,28},{8,16},{12,20},{16,8},{20,12},{24,0},{28,4},{32,56},... | collective-permute-start | bytes 245768 | tf_op jit(solution)/shard_map/ppermute | solution.py:23
  40.2 7.8 %collective-permute-start.9 = (f32[160,128]{1,0:T(8,128)S(1)}, f32[160,128]{1,0:T(8,128)S(1)}, u32[]{:S(2)}, u32[]{:S(2)}) collective-permute-start(f32[160,128]{1,0:T(8,128)S(1)} %add_add_fusion.1), channel_id=1, source_target_pairs={{0,16},{4,20},{8,24},{12,28},{16,0},{20,4},{24,8},{28,12},{32,48},... | collective-permute-start | bytes 245768 | tf_op jit(solution)/shard_map/ppermute | solution.py:23
  42.9 5.1 %collective-permute-start.8 = (f32[160,128]{1,0:T(8,128)S(1)}, f32[160,128]{1,0:T(8,128)S(1)}, u32[]{:S(2)}, u32[]{:S(2)}) collective-permute-start(f32[160,128]{1,0:T(8,128)S(1)} %add_add_fusion.1), channel_id=1, source_target_pairs={{0,8},{4,12},{8,0},{12,4},{16,24},{20,28},{24,16},{28,20},{32,40},... | collective-permute-start | bytes 245768 | tf_op jit(solution)/shard_map/ppermute | solution.py:23
  44.5 13.3 %all-to-all-start.1 = ((f32[8,24,256]{2,1,0:T(8,128)}), f32[8,24,256]{2,1,0:T(8,128)S(1)}, u32[]{:S(2)}, u32[]{:S(2)}) async-start(f32[8,24,256]{2,1,0:T(8,128)} %reduce_sum.18), calls=%async_computation.1 | async-start | bytes 393216 | tf_op jit(solution)/shard_map/all_to_all | solution.py:320
  48.0 1.5 %collective-permute-start.11 = (f32[160,128]{1,0:T(8,128)S(1)}, f32[160,128]{1,0:T(8,128)S(1)}, u32[]{:S(2)}, u32[]{:S(2)}) collective-permute-start(f32[160,128]{1,0:T(8,128)S(1)} %add_add_fusion.mine), channel_id=1, source_target_pairs={{0,4},{4,0},{8,12},{12,8},{16,20},{20,16},{24,28},{28,24},{32,36},... | collective-permute-start | bytes 245768 | tf_op jit(solution)/shard_map/ppermute | solution.py:23
  57.8 5.9 %collective-permute-start.15 = (f32[24,256]{1,0:T(8,128)S(1)}, f32[24,256]{1,0:T(8,128)S(1)}, u32[]{:S(2)}, u32[]{:S(2)}) collective-permute-start(f32[24,256]{1,0:T(8,128)S(1)} %reduce_sum.19), channel_id=1, source_target_pairs={{0,3},{1,2},{2,1},{3,0},{4,7},{5,6},{6,5},{7,4},{8,11},{9,10},{10,... | collective-permute-start | bytes 73736 | tf_op jit(solution)/shard_map/ppermute | solution.py:23
  59.3 5.3 %collective-permute-start.14 = (f32[24,256]{1,0:T(8,128)S(1)}, f32[24,256]{1,0:T(8,128)S(1)}, u32[]{:S(2)}, u32[]{:S(2)}) collective-permute-start(f32[24,256]{1,0:T(8,128)S(1)} %reduce_sum.19), channel_id=1, source_target_pairs={{0,2},{1,3},{2,0},{3,1},{4,6},{5,7},{6,4},{7,5},{8,10},{9,11},{10,... | collective-permute-start | bytes 73736 | tf_op jit(solution)/shard_map/ppermute | solution.py:23
  60.1 4.6 %collective-permute-start.13 = (f32[24,256]{1,0:T(8,128)S(1)}, f32[24,256]{1,0:T(8,128)S(1)}, u32[]{:S(2)}, u32[]{:S(2)}) collective-permute-start(f32[24,256]{1,0:T(8,128)S(1)} %reduce_sum.19), channel_id=1, source_target_pairs={{0,1},{1,0},{2,3},{3,2},{4,5},{5,4},{6,7},{7,6},{8,9},{9,8},{10,11... | collective-permute-start | bytes 73736 | tf_op jit(solution)/shard_map/ppermute | solution.py:23

commit v5 on v4

--- a/solution.py
+++ b/solution.py
@@ -232,7 +232,9 @@
     s[2 * PANEL :, :LANES] = jnp.zeros_like(corners, shape=(2 * PANEL, LANES))
 
 
-def front_kernel(core, e, t, sketch, mine, theirs, kept, given, e_kept, t_kept, sems, *, scale):
+def front_kernel(
+    core, e, t, sketch_out, mine, theirs, kept, given, e_kept, t_kept, sketch, sems, *, scale
+):
     steps = e.shape[0] // LOAD
     load_t = pltpu.make_async_copy(t, t_kept, sems.at[steps])
     load_t.start()
@@ -251,6 +253,8 @@
         sketch[rows, :] = jnp.dot(
             e_kept[rows, :], t_kept[...], preferred_element_type=jnp.float32
         ).astype(jnp.bfloat16)
+    store = pltpu.make_async_copy(sketch, sketch_out, sems.at[steps + 1])
+    store.start()
     s = sketch[...]
     by_rows = (((0,), (0,)), ((), ()))
     gram = lax.dot_general(s, s, by_rows, preferred_element_type=jnp.float32)
@@ -271,6 +275,7 @@
             for x in range(n_x):
                 kept[x, z + dz] = jnp.where(first, c[dz, x, 0], c[dz, x, 1])
                 given[x, z + dz] = jnp.where(first, c[dz, x, 1], c[dz, x, 0])
+    store.wait()
 
 
 def front(core, e, t, rows_total, n_x, n_z):
@@ -291,11 +296,12 @@
             cross_half,
         ),
         in_specs=[pl.BlockSpec(memory_space=pltpu.SMEM), hbm, hbm],
-        out_specs=(vmem,) * 5,
+        out_specs=(pl.BlockSpec(memory_space=pl.ANY),) + (vmem,) * 4,
         scratch_shapes=[
             pltpu.VMEM(e.shape, e.dtype),
             pltpu.VMEM(t.shape, t.dtype),
-            pltpu.SemaphoreType.DMA((rows // LOAD + 1,)),
+            pltpu.VMEM((rows, order), e.dtype),
+            pltpu.SemaphoreType.DMA((rows // LOAD + 2,)),
         ],
         compiler_params=pltpu.CompilerParams(vmem_limit_bytes=52 * 2**20),
     )(core, e, t)

time: 65.8 us -> 65.8 us (level)
  no operation moved by 1% of the time
where the time goes in v5:
time: 65.8 us; the launch traced here: 65.6 us
  starting transfers between devices  33.7 us (51%)
  Pallas kernels  16.5 us (25%)
  waiting for transfers between devices  11.9 us (18%)
  other arithmetic  1.83 us (3%)
  matrix products  0.94 us (1%)
  between operations  0.76 us (1%)
    ppermute x16, starting transfers between devices, shifted(): lax.ppermute(x, axis, [(i, target(i)) for i in range(lax.axis_size(axis))])  25.4 us
    ppermute x16, waiting for transfers between devices, shifted(): lax.ppermute(x, axis, [(i, target(i)) for i in range(lax.axis_size(axis))])  11.3 us
    pallas_call x1, Pallas kernels, factor(): pl.pallas_call(factor_kernel, out_shape=jax.ShapeDtypeStruct((order, orde...  7.61 us
    pallas_call x1, Pallas kernels, front(): pl.pallas_call(functools.partial(front_kernel, scale=1.0 / rows_total), o...  7.14 us
    all_to_all x1, starting transfers between devices, body(): lax.all_to_all(kept, 'wide', 0, 0, tiled=True, axis_index_groups=groups_x)  4.8 us
    all_to_all x1, starting transfers between devices, body(): lax.all_to_all(kept, 'wide', 0, 0, tiled=True, axis_index_groups=groups_z)  3.51 us
    pallas_call x1, Pallas kernels, basis_of(): pl.pallas_call(basis_kernel, out_shape=jax.ShapeDtypeStruct((rows, order)...  1.71 us
  transfers between devices with their start and end apart: 18, of which 7 were waited for; matrix products, arithmetic and copies ran while one was open for 3% of the time, Pallas kernels for 14%

profile of v5, /device:TPU:4, one launch (start us, length us, event | category | flops | bytes accessed | tf_op | source)
XLA Modules:
  0.0 65.6 jit_solution(12235534239788712302)
XLA Ops:
  0.6 7.1 %shard_map.41 = (bf16[2048,256]{1,0:T(8,128)(2,1)}, f32[160,128]{1,0:T(8,128)S(1)}, f32[160,128]{1,0:T(8,128)S(1)}, f32[4,8,24,256]{3,2,1,0:T(8,128)S(1)}, f32[4,8,24,256]{3,2,1,0:T(8,128)S(1)}) custom-call(s32[1]{0:T(128)} %bitcast.core, bf16[2048,1536]{1,0:T(8,128)(2,1)} %e.1, bf16[1536,256]{1,0:T(8,128)(2,1)} %t.1), custom_call_target="tpu_custom_call" | custom-call | tf_op jit(solution)/shard_map/pallas_call | solution.py:289
  7.9 1.3 %collective-permute-done = f32[160,128]{1,0:T(8,128)S(1)} collective-permute-done((f32[160,128]{1,0:T(8,128)S(1)}, f32[160,128]{1,0:T(8,128)S(1)}, u32[]{:S(2)}, u32[]{:S(2)}) %collective-permute-start) | collective-permute-done | bytes 81952 | tf_op jit(solution)/shard_map/ppermute | solution.py:23
  9.4 1.9 %collective-permute-start.1 = (f32[160,128]{1,0:T(8,128)S(1)}, f32[160,128]{1,0:T(8,128)S(1)}, u32[]{:S(2)}, u32[]{:S(2)}) collective-permute-start(f32[160,128]{1,0:T(8,128)S(1)} %add.45), channel_id=1, source_target_pairs={{0,32},{4,36},{8,40},{12,44},{16,48},{20,52},{24,56},{28,60},{32,0... | collective-permute-start | bytes 245768 | tf_op jit(solution)/shard_map/ppermute | solution.py:23
  11.3 3.0 %collective-permute-done.1 = f32[160,128]{1,0:T(8,128)S(1)} collective-permute-done((f32[160,128]{1,0:T(8,128)S(1)}, f32[160,128]{1,0:T(8,128)S(1)}, u32[]{:S(2)}, u32[]{:S(2)}) %collective-permute-start.1) | collective-permute-done | bytes 81952 | tf_op jit(solution)/shard_map/ppermute | solution.py:23
  14.3 6.7 %collective-permute-start.4 = (f32[160,128]{1,0:T(8,128)S(1)}, f32[160,128]{1,0:T(8,128)S(1)}, u32[]{:S(2)}, u32[]{:S(2)}) collective-permute-start(f32[160,128]{1,0:T(8,128)S(1)} %add.46), channel_id=1, source_target_pairs={{0,160},{4,164},{8,168},{12,172},{16,176},{20,180},{24,184},{28,18... | collective-permute-start | bytes 245768 | tf_op jit(solution)/shard_map/ppermute | solution.py:23
  21.5 3.1 %collective-permute-start.2 = (f32[160,128]{1,0:T(8,128)S(1)}, f32[160,128]{1,0:T(8,128)S(1)}, u32[]{:S(2)}, u32[]{:S(2)}) collective-permute-start(f32[160,128]{1,0:T(8,128)S(1)} %add.46), channel_id=1, source_target_pairs={{0,224},{4,228},{8,232},{12,236},{16,240},{20,244},{24,248},{28,25... | collective-permute-start | bytes 245768 | tf_op jit(solution)/shard_map/ppermute | solution.py:23
  24.7 1.0 %add.56 = f32[4,8,24,256]{3,2,1,0:T(8,128)} add(f32[4,8,24,256]{3,2,1,0:T(8,128)S(1)} %get-tuple-element.16, f32[4,8,24,256]{3,2,1,0:T(8,128)S(1)} %collective-permute-done.12) | non-fusion elementwise | flops 196608 | bytes 2359296 | tf_op jit(solution)/shard_map/add | solution.py:320
  25.7 4.8 %all-to-all-start = ((f32[4,8,24,256]{3,2,1,0:T(8,128)}), f32[4,8,24,256]{3,2,1,0:T(8,128)S(1)}, u32[]{:S(2)}, u32[]{:S(2)}) async-start(f32[4,8,24,256]{3,2,1,0:T(8,128)} %add.56), calls=%async_computation | async-start | bytes 1572864 | tf_op jit(solution)/shard_map/all_to_all | solution.py:321
  30.5 3.1 %collective-permute-start.7 = (f32[160,128]{1,0:T(8,128)S(1)}, f32[160,128]{1,0:T(8,128)S(1)}, u32[]{:S(2)}, u32[]{:S(2)}) collective-permute-start(f32[160,128]{1,0:T(8,128)S(1)} %add_add_fusion.2), channel_id=1, source_target_pairs={{0,3},{1,2},{2,1},{3,0},{4,7},{5,6},{6,5},{7,4},{8,11},{9,10},{10,... | collective-permute-start | bytes 245768 | tf_op jit(solution)/shard_map/ppermute | solution.py:23
  34.7 2.4 %collective-permute-done.7 = f32[160,128]{1,0:T(8,128)S(1)} collective-permute-done((f32[160,128]{1,0:T(8,128)S(1)}, f32[160,128]{1,0:T(8,128)S(1)}, u32[]{:S(2)}, u32[]{:S(2)}) %collective-permute-start.7) | collective-permute-done | bytes 81952 | tf_op jit(solution)/shard_map/ppermute | solution.py:23
  37.1 2.4 %collective-permute-done.6 = f32[160,128]{1,0:T(8,128)S(1)} collective-permute-done((f32[160,128]{1,0:T(8,128)S(1)}, f32[160,128]{1,0:T(8,128)S(1)}, u32[]{:S(2)}, u32[]{:S(2)}) %collective-permute-start.6) | collective-permute-done | bytes 81952 | tf_op jit(solution)/shard_map/ppermute | solution.py:23
  39.6 0.6 collective-permute-start.10
  40.2 2.7 %collective-permute-start.9 = (f32[160,128]{1,0:T(8,128)S(1)}, f32[160,128]{1,0:T(8,128)S(1)}, u32[]{:S(2)}, u32[]{:S(2)}) collective-permute-start(f32[160,128]{1,0:T(8,128)S(1)} %add_add_fusion.1), channel_id=1, source_target_pairs={{0,16},{4,20},{8,24},{12,28},{16,0},{20,4},{24,8},{28,12},{32,48},... | collective-permute-start | bytes 245768 | tf_op jit(solution)/shard_map/ppermute | solution.py:23
  42.9 0.9 %collective-permute-start.8 = (f32[160,128]{1,0:T(8,128)S(1)}, f32[160,128]{1,0:T(8,128)S(1)}, u32[]{:S(2)}, u32[]{:S(2)}) collective-permute-start(f32[160,128]{1,0:T(8,128)S(1)} %add_add_fusion.1), channel_id=1, source_target_pairs={{0,8},{4,12},{8,0},{12,4},{16,24},{20,28},{24,16},{28,20},{32,40},... | collective-permute-start | bytes 245768 | tf_op jit(solution)/shard_map/ppermute | solution.py:23
  43.8 0.7 %reduce_sum.18 = f32[8,24,256]{2,1,0:T(8,128)} reduce(f32[4,8,24,256]{3,2,1,0:T(8,128)S(1)} %all-to-all-done, f32[]{:T(128)} %constant.11.clone.1), dimensions={0}, to_apply=%region_0.0 | reduce | flops 147456 | bytes 983044 | tf_op jit(solution)/shard_map/reduce_sum | solution.py:325
  44.5 3.5 %all-to-all-start.1 = ((f32[8,24,256]{2,1,0:T(8,128)}), f32[8,24,256]{2,1,0:T(8,128)S(1)}, u32[]{:S(2)}, u32[]{:S(2)}) async-start(f32[8,24,256]{2,1,0:T(8,128)} %reduce_sum.18), calls=%async_computation.1 | async-start | bytes 393216 | tf_op jit(solution)/shard_map/all_to_all | solution.py:326
  48.3 1.3 %collective-permute-done.11.other = f32[160,128]{1,0:T(8,128)S(1)} collective-permute-done((f32[160,128]{1,0:T(8,128)S(1)}, f32[160,128]{1,0:T(8,128)S(1)}, u32[]{:S(2)}, u32[]{:S(2)}) %collective-permute-start.11) | collective-permute-done | bytes 81952 | tf_op jit(solution)/shard_map/ppermute | solution.py:23
  49.6 7.6 %shard_map.42.inv_t = f32[256,256]{1,0:T(8,128)S(1)} custom-call(s32[1]{0:T(128)} %bitcast.core, f32[160,128]{1,0:T(8,128)S(1)} %add_add_fusion.mine, f32[160,128]{1,0:T(8,128)S(1)} %collective-permute-done.11.other), custom_call_target="tpu_custom_call" | custom-call | bytes 20971520 | tf_op jit(solution)/shard_map/pallas_call | solution.py:165
  57.8 1.5 %collective-permute-start.15 = (f32[24,256]{1,0:T(8,128)S(1)}, f32[24,256]{1,0:T(8,128)S(1)}, u32[]{:S(2)}, u32[]{:S(2)}) collective-permute-start(f32[24,256]{1,0:T(8,128)S(1)} %reduce_sum.19), channel_id=1, source_target_pairs={{0,3},{1,2},{2,1},{3,0},{4,7},{5,6},{6,5},{7,4},{8,11},{9,10},{10,... | collective-permute-start | bytes 73736 | tf_op jit(solution)/shard_map/ppermute | solution.py:23
  59.3 0.8 %collective-permute-start.14 = (f32[24,256]{1,0:T(8,128)S(1)}, f32[24,256]{1,0:T(8,128)S(1)}, u32[]{:S(2)}, u32[]{:S(2)}) collective-permute-start(f32[24,256]{1,0:T(8,128)S(1)} %reduce_sum.19), channel_id=1, source_target_pairs={{0,2},{1,3},{2,0},{3,1},{4,6},{5,7},{6,4},{7,5},{8,10},{9,11},{10,... | collective-permute-start | bytes 73736 | tf_op jit(solution)/shard_map/ppermute | solution.py:23
  60.1 1.9 %collective-permute-start.13 = (f32[24,256]{1,0:T(8,128)S(1)}, f32[24,256]{1,0:T(8,128)S(1)}, u32[]{:S(2)}, u32[]{:S(2)}) collective-permute-start(f32[24,256]{1,0:T(8,128)S(1)} %reduce_sum.19), channel_id=1, source_target_pairs={{0,1},{1,0},{2,3},{3,2},{4,5},{5,4},{6,7},{7,6},{8,9},{9,8},{10,11... | collective-permute-start | bytes 73736 | tf_op jit(solution)/shard_map/ppermute | solution.py:23
  62.0 1.7 %shard_map.43 = f32[2048,256]{1,0:T(8,128)} custom-call(bf16[2048,256]{1,0:T(8,128)(2,1)S(1)} %copy-done, f32[256,256]{1,0:T(8,128)S(1)} %shard_map.42.inv_t), custom_call_target="tpu_custom_call" | custom-call | flops 536870912 | bytes 3145728 | tf_op jit(solution)/shard_map/pallas_call | solution.py:200
  63.7 0.9 %collective-permute-done.14 = f32[24,256]{1,0:T(8,128)S(1)} collective-permute-done((f32[24,256]{1,0:T(8,128)S(1)}, f32[24,256]{1,0:T(8,128)S(1)}, u32[]{:S(2)}, u32[]{:S(2)}) %collective-permute-start.14) | collective-permute-done | bytes 24608 | tf_op jit(solution)/shard_map/ppermute | solution.py:23
  64.7 0.9 %convolution_multiply_fusion = f32[24,256]{1,0:T(8,128)} fusion(f32[256,256]{1,0:T(8,128)S(1)} %shard_map.42.inv_t, f32[24,256]{1,0:T(8,128)S(1)} %collective-permute-done.14, f32[24,256]{1,0:T(8,128)S(1)} %collective-permute-done.15, f32[24,256]{1,0:T(8,128)S(1)} %reduce_sum.19, f32[24,256]{1,0:T(8,128)S(1)} %collective-permute-done.13), kind=kOutput, calls=%fused_computation | convolution fusion | flops 18898944 | bytes 385024 | tf_op jit(solution)/shard_map/dot_general | solution.py:339
  (26 shorter events, 2.9 us)
Async XLA Ops:
  7.8 54.2 %copy-start = (bf16[2048,256]{1,0:T(8,128)(2,1)S(1)}, bf16[2048,256]{1,0:T(8,128)(2,1)}, u32[]{:S(2)}) copy-start(bf16[2048,256]{1,0:T(8,128)(2,1)} %get-tuple-element.11.sketch) | copy-start | bytes 3145732
  7.8 1.4 %collective-permute-start = (f32[160,128]{1,0:T(8,128)S(1)}, f32[160,128]{1,0:T(8,128)S(1)}, u32[]{:S(2)}, u32[]{:S(2)}) collective-permute-start(f32[160,128]{1,0:T(8,128)S(1)} %get-tuple-element.13), channel_id=1, source_target_pairs={{0,4},{4,0},{8,12},{12,8},{16,20},{20,16},{24,28},{28,24},{32,36},... | collective-permute-start | bytes 245768 | tf_op jit(solution)/shard_map/ppermute | solution.py:23
  9.2 15.5 %collective-permute-start.12 = (f32[4,8,24,256]{3,2,1,0:T(8,128)S(1)}, f32[4,8,24,256]{3,2,1,0:T(8,128)S(1)}, u32[]{:S(2)}, u32[]{:S(2)}) collective-permute-start(f32[4,8,24,256]{3,2,1,0:T(8,128)S(1)} %get-tuple-element.17), channel_id=1, source_target_pairs={{0,4},{4,0},{8,12},{12,8},{16,20},{20,16},{24,28},{28,24},{32,36},... | collective-permute-start | bytes 2359304 | tf_op jit(solution)/shard_map/ppermute | solution.py:23
  9.4 4.9 %collective-permute-start.1 = (f32[160,128]{1,0:T(8,128)S(1)}, f32[160,128]{1,0:T(8,128)S(1)}, u32[]{:S(2)}, u32[]{:S(2)}) collective-permute-start(f32[160,128]{1,0:T(8,128)S(1)} %add.45), channel_id=1, source_target_pairs={{0,32},{4,36},{8,40},{12,44},{16,48},{20,52},{24,56},{28,60},{32,0... | collective-permute-start | bytes 245768 | tf_op jit(solution)/shard_map/ppermute | solution.py:23
  14.3 16.1 %collective-permute-start.4 = (f32[160,128]{1,0:T(8,128)S(1)}, f32[160,128]{1,0:T(8,128)S(1)}, u32[]{:S(2)}, u32[]{:S(2)}) collective-permute-start(f32[160,128]{1,0:T(8,128)S(1)} %add.46), channel_id=1, source_target_pairs={{0,160},{4,164},{8,168},{12,172},{16,176},{20,180},{24,184},{28,18... | collective-permute-start | bytes 245768 | tf_op jit(solution)/shard_map/ppermute | solution.py:23
  21.0 9.5 %collective-permute-start.3 = (f32[160,128]{1,0:T(8,128)S(1)}, f32[160,128]{1,0:T(8,128)S(1)}, u32[]{:S(2)}, u32[]{:S(2)}) collective-permute-start(f32[160,128]{1,0:T(8,128)S(1)} %add.46), channel_id=1, source_target_pairs={{0,192},{4,196},{8,200},{12,204},{16,208},{20,212},{24,216},{28,22... | collective-permute-start | bytes 245768 | tf_op jit(solution)/shard_map/ppermute | solution.py:23
  21.5 8.9 %collective-permute-start.2 = (f32[160,128]{1,0:T(8,128)S(1)}, f32[160,128]{1,0:T(8,128)S(1)}, u32[]{:S(2)}, u32[]{:S(2)}) collective-permute-start(f32[160,128]{1,0:T(8,128)S(1)} %add.46), channel_id=1, source_target_pairs={{0,224},{4,228},{8,232},{12,236},{16,240},{20,244},{24,248},{28,25... | collective-permute-start | bytes 245768 | tf_op jit(solution)/shard_map/ppermute | solution.py:23
  25.7 18.1 %all-to-all-start = ((f32[4,8,24,256]{3,2,1,0:T(8,128)}), f32[4,8,24,256]{3,2,1,0:T(8,128)S(1)}, u32[]{:S(2)}, u32[]{:S(2)}) async-start(f32[4,8,24,256]{3,2,1,0:T(8,128)} %add.56), calls=%async_computation | async-start | bytes 1572864 | tf_op jit(solution)/shard_map/all_to_all | solution.py:321
  30.5 6.6 %collective-permute-start.7 = (f32[160,128]{1,0:T(8,128)S(1)}, f32[160,128]{1,0:T(8,128)S(1)}, u32[]{:S(2)}, u32[]{:S(2)}) collective-permute-start(f32[160,128]{1,0:T(8,128)S(1)} %add_add_fusion.2), channel_id=1, source_target_pairs={{0,3},{1,2},{2,1},{3,0},{4,7},{5,6},{6,5},{7,4},{8,11},{9,10},{10,... | collective-permute-start | bytes 245768 | tf_op jit(solution)/shard_map/ppermute | solution.py:23
  33.6 5.9 %collective-permute-start.6 = (f32[160,128]{1,0:T(8,128)S(1)}, f32[160,128]{1,0:T(8,128)S(1)}, u32[]{:S(2)}, u32[]{:S(2)}) collective-permute-start(f32[160,128]{1,0:T(8,128)S(1)} %add_add_fusion.2), channel_id=1, source_target_pairs={{0,2},{1,3},{2,0},{3,1},{4,6},{5,7},{6,4},{7,5},{8,10},{9,11},{10,... | collective-permute-start | bytes 245768 | tf_op jit(solution)/shard_map/ppermute | solution.py:23
  34.2 5.3 %collective-permute-start.5 = (f32[160,128]{1,0:T(8,128)S(1)}, f32[160,128]{1,0:T(8,128)S(1)}, u32[]{:S(2)}, u32[]{:S(2)}) collective-permute-start(f32[160,128]{1,0:T(8,128)S(1)} %add_add_fusion.2), channel_id=1, source_target_pairs={{0,1},{1,0},{2,3},{3,2},{4,5},{5,4},{6,7},{7,6},{8,9},{9,8},{10,11... | collective-permute-start | bytes 245768 | tf_op jit(solution)/shard_map/ppermute | solution.py:23
  39.6 8.4 %collective-permute-start.10 = (f32[160,128]{1,0:T(8,128)S(1)}, f32[160,128]{1,0:T(8,128)S(1)}, u32[]{:S(2)}, u32[]{:S(2)}) collective-permute-start(f32[160,128]{1,0:T(8,128)S(1)} %add_add_fusion.1), channel_id=1, source_target_pairs={{0,24},{4,28},{8,16},{12,20},{16,8},{20,12},{24,0},{28,4},{32,56},... | collective-permute-start | bytes 245768 | tf_op jit(solution)/shard_map/ppermute | solution.py:23
  40.2 7.8 %collective-permute-start.9 = (f32[160,128]{1,0:T(8,128)S(1)}, f32[160,128]{1,0:T(8,128)S(1)}, u32[]{:S(2)}, u32[]{:S(2)}) collective-permute-start(f32[160,128]{1,0:T(8,128)S(1)} %add_add_fusion.1), channel_id=1, source_target_pairs={{0,16},{4,20},{8,24},{12,28},{16,0},{20,4},{24,8},{28,12},{32,48},... | collective-permute-start | bytes 245768 | tf_op jit(solution)/shard_map/ppermute | solution.py:23
  42.9 5.1 %collective-permute-start.8 = (f32[160,128]{1,0:T(8,128)S(1)}, f32[160,128]{1,0:T(8,128)S(1)}, u32[]{:S(2)}, u32[]{:S(2)}) collective-permute-start(f32[160,128]{1,0:T(8,128)S(1)} %add_add_fusion.1), channel_id=1, source_target_pairs={{0,8},{4,12},{8,0},{12,4},{16,24},{20,28},{24,16},{28,20},{32,40},... | collective-permute-start | bytes 245768 | tf_op jit(solution)/shard_map/ppermute | solution.py:23
  44.5 13.3 %all-to-all-start.1 = ((f32[8,24,256]{2,1,0:T(8,128)}), f32[8,24,256]{2,1,0:T(8,128)S(1)}, u32[]{:S(2)}, u32[]{:S(2)}) async-start(f32[8,24,256]{2,1,0:T(8,128)} %reduce_sum.18), calls=%async_computation.1 | async-start | bytes 393216 | tf_op jit(solution)/shard_map/all_to_all | solution.py:326
  48.0 1.5 %collective-permute-start.11 = (f32[160,128]{1,0:T(8,128)S(1)}, f32[160,128]{1,0:T(8,128)S(1)}, u32[]{:S(2)}, u32[]{:S(2)}) collective-permute-start(f32[160,128]{1,0:T(8,128)S(1)} %add_add_fusion.mine), channel_id=1, source_target_pairs={{0,4},{4,0},{8,12},{12,8},{16,20},{20,16},{24,28},{28,24},{32,36},... | collective-permute-start | bytes 245768 | tf_op jit(solution)/shard_map/ppermute | solution.py:23
  57.8 5.9 %collective-permute-start.15 = (f32[24,256]{1,0:T(8,128)S(1)}, f32[24,256]{1,0:T(8,128)S(1)}, u32[]{:S(2)}, u32[]{:S(2)}) collective-permute-start(f32[24,256]{1,0:T(8,128)S(1)} %reduce_sum.19), channel_id=1, source_target_pairs={{0,3},{1,2},{2,1},{3,0},{4,7},{5,6},{6,5},{7,4},{8,11},{9,10},{10,... | collective-permute-start | bytes 73736 | tf_op jit(solution)/shard_map/ppermute | solution.py:23
  59.3 5.3 %collective-permute-start.14 = (f32[24,256]{1,0:T(8,128)S(1)}, f32[24,256]{1,0:T(8,128)S(1)}, u32[]{:S(2)}, u32[]{:S(2)}) collective-permute-start(f32[24,256]{1,0:T(8,128)S(1)} %reduce_sum.19), channel_id=1, source_target_pairs={{0,2},{1,3},{2,0},{3,1},{4,6},{5,7},{6,4},{7,5},{8,10},{9,11},{10,... | collective-permute-start | bytes 73736 | tf_op jit(solution)/shard_map/ppermute | solution.py:23
  60.1 4.6 %collective-permute-start.13 = (f32[24,256]{1,0:T(8,128)S(1)}, f32[24,256]{1,0:T(8,128)S(1)}, u32[]{:S(2)}, u32[]{:S(2)}) collective-permute-start(f32[24,256]{1,0:T(8,128)S(1)} %reduce_sum.19), channel_id=1, source_target_pairs={{0,1},{1,0},{2,3},{3,2},{4,5},{5,4},{6,7},{7,6},{8,9},{9,8},{10,11... | collective-permute-start | bytes 73736 | tf_op jit(solution)/shard_map/ppermute | solution.py:23
